TPU v7x, 512 devices: a whole 4x4x16 slice. The times are simulated.
512 devices in a mesh: req: 32 (over z, core), exp: 16 (over y, x).
Axes of the slice: x: 4, y: 4, z: 16, core: 2. Of those that a mesh axis runs over, the one named last changes fastest.
Arguments:
- queries: bfloat16 [256, 8192], P('req'), may hold values from -80 to 80
- new_keys: bfloat16 [256, 512], P('req'), may hold values from -12 to 12
- new_values: bfloat16 [256, 512], P('req'), may hold values from -18 to 18
- key_cache: bfloat16 [64, 384, 16, 512], P('req', None, 'exp'), may hold values from -12 to 12
- value_cache: bfloat16 [64, 384, 16, 512], P('req', None, 'exp'), may hold values from -18 to 18
- lengths: int32 [64], replicated, may hold values from 1 to 6144, as said below
- out_proj: bfloat16 [8192, 4096], P('exp', 'req'), may hold values from -0.0625 to 0.0625
- residual: bfloat16 [256, 4096], P(None, 'req'), may hold values from -6 to 6
- norm_gain: float32 [4096], P('req'), may hold values from 0.5 to 1.5
- gate_weight: bfloat16 [32, 4096, 1536], P('exp', 'req'), may hold values from -0.09375 to 0.09375
- up_weight: bfloat16 [32, 4096, 1536], P('exp', 'req'), may hold values from -0.09375 to 0.09375
- down_weight: bfloat16 [32, 1536, 4096], P('exp', None, 'req'), may hold values from -0.15625 to 0.15625
- expert_ids: int32 [256, 8], replicated, may hold values from 0 to 31, all different within a row; in each aligned block of 256 rows (0 to 255, 256 to 511, ...) at most 128 rows name the same one
- route_weights: float32 [256, 8], replicated, may hold values from 0.1 to 1
Outputs:
- layer_out: bfloat16 [256, 4096], P('exp', 'req')
Inputs may be any that keep to these rules, and one draw needn't show every extreme that they name: `lengths`: some request has exactly 6144 cached tokens. `expert_ids`: each row names 8 different experts; no expert is named by more than 128 rows, a bound that some block reaches.
All inputs are finite; a program needn't handle non-finite values.
Results may differ from a plain program's by a relative error of at most 0.014.
Values may be sent and summed in bfloat16 or wider, within the bound.
A program may use at most 64 MiB of HBM per device.

v0:
```python
import jax
import jax.numpy as jnp
from jax import lax
from jax.sharding import PartitionSpec as P

D = 4096
QH = 64
KVH = 4
HD = 128
TOP = 8
EXP_DEV = 2
SLOTS = 2
STEPS = 4


neg_big = -1e30
norm_eps = 1e-06


def merged_2(part, axis, combine):
    gathered = jax.tree.map(lambda a: lax.all_gather(a, axis), part)

    def take(source):
        return jax.tree.map(lambda a: lax.dynamic_index_in_dim(a, source, 0, False), gathered)

    return lax.fori_loop(
        1, lax.axis_size(axis), lambda source, state: combine(state, take(source)), take(0)
    )


def combine_parts(first, second):
    first_max, first_sum, first_acc = first
    second_max, second_sum, second_acc = second
    top_max = jnp.maximum(first_max, second_max)
    first_scale = jnp.exp(first_max - top_max)
    second_scale = jnp.exp(second_max - top_max)
    return (
        top_max,
        first_sum * first_scale + second_sum * second_scale,
        first_acc * first_scale[..., None] + second_acc * second_scale[..., None],
    )


def cache_part(query_grid, slot_keys, slot_values, valid_count):
    block_rows = min(128, slot_keys.shape[0])
    steps_n = query_grid.shape[0]
    group_n = query_grid.shape[2]
    head_scale = HD ** (-0.5)
    start_state = (
        jnp.full((KVH, steps_n, group_n), neg_big, jnp.float32),
        jnp.zeros((KVH, steps_n, group_n), jnp.float32),
        jnp.zeros((KVH, steps_n, group_n, HD), jnp.float32),
    )
    block_count = (valid_count + block_rows - 1) // block_rows

    def visit(block_no, carried):
        first_row = block_no * block_rows
        key_block = lax.dynamic_slice_in_dim(slot_keys, first_row, block_rows, 0).reshape(
            block_rows, KVH, HD
        )
        value_block = lax.dynamic_slice_in_dim(slot_values, first_row, block_rows, 0).reshape(
            block_rows, KVH, HD
        )
        scores = (
            jnp.einsum("tgjd,kgd->gtjk", query_grid, key_block, preferred_element_type=jnp.float32)
            * head_scale
        )
        live_keys = first_row + jnp.arange(block_rows, dtype=jnp.int32) < valid_count
        scores = jnp.where(live_keys, scores, neg_big)
        old_max, old_sum, old_acc = carried
        new_max = jnp.maximum(old_max, jnp.max(scores, axis=-1))
        weights = jnp.where(live_keys, jnp.exp(scores - new_max[..., None]), 0.0)
        rescale = jnp.exp(old_max - new_max)
        new_sum = old_sum * rescale + jnp.sum(weights, axis=-1)
        new_acc = old_acc * rescale[..., None] + jnp.einsum(
            "gtjk,kgd->gtjd",
            weights.astype(jnp.bfloat16),
            value_block,
            preferred_element_type=jnp.float32,
        )
        return (new_max, new_sum, new_acc)

    return lax.fori_loop(0, block_count, visit, start_state)


def fresh_part(query_grid, fresh_keys, fresh_values):
    steps_n = query_grid.shape[0]
    key_grid = fresh_keys.reshape(steps_n, KVH, HD)
    value_grid = fresh_values.reshape(steps_n, KVH, HD)
    scores = jnp.einsum(
        "tgjd,sgd->gtjs", query_grid, key_grid, preferred_element_type=jnp.float32
    ) * HD ** (-0.5)
    causal = jnp.arange(steps_n)[:, None] >= jnp.arange(steps_n)[None, :]
    scores = jnp.where(causal[None, :, None, :], scores, neg_big)
    fresh_max = jnp.max(scores, axis=-1)
    weights = jnp.where(causal[None, :, None, :], jnp.exp(scores - fresh_max[..., None]), 0.0)
    return (
        fresh_max,
        jnp.sum(weights, axis=-1),
        jnp.einsum(
            "gtjs,sgd->gtjd",
            weights.astype(jnp.bfloat16),
            value_grid,
            preferred_element_type=jnp.float32,
        ),
    )


def activate(gate_sum, up_sum, square_sum):
    norm_scale = lax.rsqrt(square_sum / D + norm_eps)[..., None]
    return (jax.nn.silu(norm_scale * gate_sum) * (norm_scale * up_sum)).astype(jnp.bfloat16)


def body(
    queries,
    new_keys,
    new_values,
    key_cache,
    value_cache,
    lengths,
    out_proj,
    residual,
    norm_gain,
    gate_weight,
    up_weight,
    down_weight,
    expert_ids,
    route_weights,
):
    req_count = lax.axis_size("req")
    exp_count = lax.axis_size("exp")
    req_rank = lax.axis_index("req")
    exp_rank = lax.axis_index("exp")
    group_n = QH // KVH
    kv_width = KVH * HD
    slot_keys = key_cache[:, :, 0, :]
    slot_values = value_cache[:, :, 0, :]
    slot_queries = queries.reshape(SLOTS, STEPS, QH * HD)
    fresh_keys = new_keys.reshape(SLOTS, STEPS, kv_width)
    fresh_values = new_values.reshape(SLOTS, STEPS, kv_width)
    holders = jnp.arange(req_count * SLOTS, dtype=jnp.int32).reshape(req_count, SLOTS)
    my_requests = lax.dynamic_index_in_dim(holders, req_rank, 0, keepdims=False)
    my_lengths = lengths[my_requests]
    query_grids = slot_queries.reshape(SLOTS, STEPS, KVH, group_n, HD)
    slot_states = []
    for slot_no in range(SLOTS):
        valid_count = jnp.maximum((my_lengths[slot_no] - exp_rank + exp_count - 1) // exp_count, 0)
        slot_states.append(
            cache_part(query_grids[slot_no], slot_keys[slot_no], slot_values[slot_no], valid_count)
        )
    stacked = tuple(
        (jnp.stack([slot_state[member] for slot_state in slot_states]) for member in range(3))
    )
    merged = merged_2(stacked, "exp", combine_parts)
    fresh = jax.vmap(fresh_part)(query_grids, fresh_keys, fresh_values)
    final_max, final_sum, final_acc = combine_parts(merged, fresh)
    attention = (
        (final_acc / final_sum[..., None])
        .transpose(0, 2, 1, 3, 4)
        .reshape(SLOTS * STEPS, QH * HD)
        .astype(jnp.bfloat16)
    )
    head_width = out_proj.shape[0]
    head_cols = lax.dynamic_slice_in_dim(attention, exp_rank * head_width, head_width, 1)
    projected = jnp.dot(
        lax.all_gather(head_cols, "req", axis=0, tiled=True),
        out_proj,
        preferred_element_type=jnp.float32,
    )
    tokens_all = req_count * SLOTS * STEPS
    held_flat = holders.reshape(-1)
    request_ids = jnp.arange(held_flat.shape[0], dtype=jnp.int32)
    position = jnp.sum(
        jnp.where(held_flat[None, :] == request_ids[:, None], request_ids[None, :], 0), axis=1
    )
    projected = projected.reshape(req_count * SLOTS, STEPS, -1)[position].reshape(tokens_all, -1)
    projected = lax.psum(projected, "exp")
    hidden_state = residual.astype(jnp.float32) + projected
    square_part = jnp.sum(hidden_state * hidden_state, axis=1)
    normed = (hidden_state * norm_gain).astype(jnp.bfloat16)
    route_cap = min(tokens_all, 2 * tokens_all * TOP // (EXP_DEV * exp_count))
    token_ids = jnp.arange(tokens_all, dtype=jnp.int32)
    slot_ids = jnp.arange(route_cap, dtype=jnp.int32)
    selectors = []
    row_weights = []
    gate_list = []
    up_list = []
    square_list = []
    for expert_no in range(EXP_DEV):
        expert_id = exp_rank * EXP_DEV + expert_no
        matches = expert_ids == expert_id
        weight_row = jnp.sum(jnp.where(matches, route_weights, 0.0), axis=1)
        routed = jnp.any(matches, axis=1)
        rank_in = jnp.cumsum(routed.astype(jnp.int32)) - 1
        selector = routed[None, :] & (rank_in[None, :] == slot_ids[:, None])
        chosen = jnp.sum(jnp.where(selector, token_ids[None, :], 0), axis=1)
        filled = jnp.any(selector, axis=1)
        rows_in = normed[chosen]
        gate_list.append(
            jnp.dot(rows_in, gate_weight[expert_no], preferred_element_type=jnp.float32)
        )
        up_list.append(jnp.dot(rows_in, up_weight[expert_no], preferred_element_type=jnp.float32))
        square_list.append(square_part[chosen])
        row_weights.append(jnp.where(filled, weight_row[chosen], 0.0))
        selectors.append(selector.astype(jnp.float32))
    gate_terms = jnp.stack(gate_list)
    up_terms = jnp.stack(up_list)
    square_terms = jnp.stack(square_list)
    gate_sum, up_sum, square_sum = lax.psum((gate_terms, up_terms, square_terms), "req")
    activated = activate(gate_sum, up_sum, square_sum)
    moe_local = jnp.zeros(hidden_state.shape, jnp.float32)
    for expert_no in range(EXP_DEV):
        expert_rows = jnp.dot(
            activated[expert_no], down_weight[expert_no], preferred_element_type=jnp.float32
        )
        weighted = row_weights[expert_no][:, None] * expert_rows
        moe_local = moe_local + jnp.dot(
            selectors[expert_no].T,
            weighted,
            precision=lax.Precision.HIGHEST,
            preferred_element_type=jnp.float32,
        )
    block_rows = tokens_all // exp_count
    summed = lax.psum_scatter(moe_local, "exp", scatter_dimension=0, tiled=True)
    base_rows = lax.dynamic_slice_in_dim(hidden_state, exp_rank * block_rows, block_rows, 0)
    return (base_rows + summed).astype(jnp.bfloat16)


def solution(mesh):
    in_specs = (
        P("req", None),
        P("req", None),
        P("req", None),
        P("req", None, "exp", None),
        P("req", None, "exp", None),
        P(),
        P("exp", "req"),
        P(None, "req"),
        P("req"),
        P("exp", "req", None),
        P("exp", "req", None),
        P("exp", None, "req"),
        P(),
        P(),
    )
    out_specs = P("exp", "req")
    return jax.shard_map(body, mesh=mesh, in_specs=in_specs, out_specs=out_specs, check_vma=False)
```

profile of v0, /device:TPU:1, one launch (start us, length us, event | category | flops | bytes accessed | tf_op | source)
XLA Modules:
  0.0 600.3 jit_solution(2144547170569574037)
XLA Ops:
  6.6 1.4 gather_fusion
  7.9 0.7 fusion.75
  9.9 1.0 slice_bitcast_fusion.5
  11.5 0.6 copy-done.2
  12.5 2.5 while.47
  15.3 0.8 while.48
  16.2 0.7 pad_maximum_fusion.2
  18.0 19.4 %all-gather.1 = f32[32,4,4,16]{3,2,1,0:T(4,128)S(1)} all-gather(f32[2,4,4,16]{3,2,1,0:T(4,128)S(1)} %pad_maximum_fusion.4), channel_id=3, replica_groups=mesh['req'=32,'exp'=16] {'exp'}, dimensions={0}, use_global_device_ids=true | all-gather | bytes 34816 | tf_op jit(solution)/shard_map/all_gather | solution.py:21
  37.4 19.2 %all-gather = f32[32,4,4,16]{3,2,1,0:T(4,128)S(1)} all-gather(f32[2,4,4,16]{3,2,1,0:T(4,128)S(1)} %pad_maximum_fusion.3), channel_id=2, replica_groups=mesh['req'=32,'exp'=16] {'exp'}, dimensions={0}, use_global_device_ids=true | all-gather | bytes 34816 | tf_op jit(solution)/shard_map/all_gather | solution.py:21
  57.3 0.4 fusion.76
  57.9 31.6 %all-gather.5.cloned.1.call-done = f32[32,4,4,16,128]{4,3,2,1,0:T(8,128)} async-done(((f32[2,4,4,16,128]{4,3,2,1,0:T(8,128)}), f32[32,4,4,16,128]{4,3,2,1,0:T(8,128)}) %all-gather.5.cloned.1.call-update) | async-done | bytes 4194320 | tf_op jit(solution)/shard_map/all_gather | solution.py:21
  89.6 1.0 slice.112
  90.5 19.3 %while.49 = (s32[]{:T(128)}, f32[2,4,4,16]{3,2,1,0:T(4,128)S(1)}, f32[2,4,4,16]{3,2,1,0:T(4,128)S(1)}, f32[2,4,4,16,128]{4,3,2,1,0:T(8,128)S(1)}, f32[16,2,4,4,1...) while((s32[]{:T(128)}, f32[2,4,4,16]{3,2,1,0:T(4,128)S(1)}, ...), condition=%wide.region_9.10_spmd, body=%wide.region_8.9_spmd.sunk | while | flops 199685 | bytes 807055 | solution.py:26
  90.6 1.2 fusion.119
  91.9 1.2 fusion.119
  93.2 1.2 fusion.119
  94.5 1.2 fusion.119
  95.8 1.2 fusion.119
  97.0 1.2 fusion.119
  98.3 1.2 fusion.119
  99.6 1.2 fusion.119
  100.9 1.2 fusion.119
  102.2 1.2 fusion.119
  103.5 1.2 fusion.119
  104.8 1.2 fusion.119
  106.1 1.2 fusion.119
  107.4 1.2 fusion.119
  108.6 1.2 fusion.119
  109.9 0.4 fusion.24
  110.5 32.4 %all_gather.27 = bf16[256,512]{1,0:T(8,128)(2,1)S(1)} all-gather(bf16[8,512]{1,0:T(8,128)(2,1)S(1)} %constant_dynamic-slice_fusion.4), channel_id=1, replica_groups=mesh['req'=32,'exp'=16] {'req'}, dimensions={0}, use_global_device_ids=true | all-gather | bytes 270336 | tf_op jit(solution)/shard_map/all_gather | solution.py:166
  143.1 1.3 gather_fusion.1
  144.5 107.2 %all-reduce.6.cloned.1.call-done = f32[256,128]{1,0:T(8,128)} async-done(((f32[256,128]{1,0:T(8,128)}), f32[256,128]{1,0:T(8,128)}) %all-reduce.6.cloned.1.call-update) | async-done | bytes 131088 | tf_op jit(solution)/shard_map/psum | solution.py:177
  251.7 1.0 multiply_reduce_fusion
  252.7 0.7 gather_fusion.6
  253.5 0.7 gather_fusion.5
  255.2 1.3 pad_maximum_fusion
  256.5 1.3 pad_maximum_fusion.1
  257.8 1.3 gather_fusion.2
  259.1 1.3 gather_fusion.7
  260.6 1.3 gather_fusion.4
  261.9 1.3 gather_fusion.3
  263.2 48.6 %psum.29 = f32[2,128]{1,0:T(2,128)S(1)} all-reduce(f32[2,128]{1,0:T(2,128)S(1)} %pad_maximum_fusion.5), channel_id=1, replica_groups=mesh['req'=32,'exp'=16] {'req'}, use_global_device_ids=true, to_apply=%region_25.26 | all-reduce | flops 256 | bytes 2048 | tf_op jit(solution)/shard_map/psum | solution.py:209
  311.8 165.1 %all-reduce.10.cloned.1.call-done = (f32[2,128,1536]{2,1,0:T(8,128)}, f32[2,128,1536]{2,1,0:T(8,128)}) async-done(((f32[2,128,1536]{2,1,0:T(8,128)}, f32[2,128,1536]{2,1,0:T(8,128)}), (f32[2,128,1536]{2,1,0:T(8,128)}, f32[2,128,1536]{2,1,0:T(8,128)})) %all-reduce.10.cloned.1.call-update) | async-done | bytes 3145744 | tf_op jit(solution)/shard_map/psum | solution.py:209
  476.9 2.5 multiply_convert_fusion
  480.3 0.9 convolution_add_fusion.2
  481.2 1.3 dynamic-slice
  483.2 109.4 %all-reduce.8.cloned.1.call-done = f32[256,128]{1,0:T(8,128)} async-done(((f32[256,128]{1,0:T(8,128)}), f32[256,128]{1,0:T(8,128)}) %all-reduce.8.cloned.1.call-update) | async-done | bytes 131088
  592.5 1.3 fusion.59
  (149 shorter events, 9.2 us)
Async XLA Ops:
  6.5 136.3 %copy-start = (bf16[512,128]{1,0:T(8,128)(2,1)S(1)}, bf16[512,128]{1,0:T(8,128)(2,1)}, u32[]{:S(2)}) copy-start(bf16[512,128]{1,0:T(8,128)(2,1)} %param.26) | copy-start | bytes 393220
  6.5 4.5 copy-start.1
  6.5 83.0 %all-gather.5.cloned.1.call-start = ((), (), s32[]{:S(2)}) async-start(), calls=%async_computation.1 | async-start | bytes 4456448 | tf_op jit(solution)/shard_map/all_gather | solution.py:21
  11.0 1.1 copy-start.2
  15.3 1.7 copy-start.7
  15.3 1.7 copy-start.8
  15.3 2.6 copy-start.9
  15.3 2.6 copy-start.10
  15.3 2.6 copy-start.5
  16.9 234.8 %all-reduce.6.cloned.1.call-start = ((), (), s32[]{:S(2)}) async-start(), calls=%async_computation | async-start | bytes 262144 | tf_op jit(solution)/shard_map/psum | solution.py:177
  109.9 141.8 %copy-start.6 = (bf16[256,128]{1,0:T(8,128)(2,1)S(1)}, bf16[256,128]{1,0:T(8,128)(2,1)}, u32[]{:S(2)}) copy-start(bf16[256,128]{1,0:T(8,128)(2,1)} %param.27) | copy-start | bytes 196612
  109.9 142.8 %copy-start.11 = (f32[128]{0:T(128)S(1)}, f32[128]{0:T(128)}, u32[]{:S(2)}) copy-start(f32[128]{0:T(128)} %param.28) | copy-start | bytes 1540
  110.4 143.8 %copy-start.3 = (bf16[2,128,1536]{2,1,0:T(8,128)(2,1)S(1)}, bf16[2,128,1536]{2,1,0:T(8,128)(2,1)}, u32[]{:S(2)}) copy-start(bf16[2,128,1536]{2,1,0:T(8,128)(2,1)} %param.29) | copy-start | bytes 2359300
  142.8 111.6 %copy-start.4 = (bf16[2,128,1536]{2,1,0:T(8,128)(2,1)S(1)}, bf16[2,128,1536]{2,1,0:T(8,128)(2,1)}, u32[]{:S(2)}) copy-start(bf16[2,128,1536]{2,1,0:T(8,128)(2,1)} %param.30) | copy-start | bytes 2359300
  144.4 332.5 %all-reduce.10.cloned.1.call-start = ((), (), s32[]{:S(2)}) async-start(), calls=%async_computation.3 | async-start | bytes 6291456 | tf_op jit(solution)/shard_map/psum | solution.py:209
  257.8 334.7 %all-reduce.8.cloned.1.call-start = ((), (), s32[]{:S(2)}) async-start(), calls=%async_computation.2 | async-start | bytes 262144
  476.9 2.5 copy-start.12
Sparse Core Ops, SparseCore 0:
  17.1 72.4 all-gather.4
  144.5 107.1 all-reduce.5
  257.9 218.9 all-reduce.9
  481.4 111.1 all-reduce.7
where the time goes:
time: 602 us; the launch traced here: 600 us
  waiting for transfers between devices  413 us (69%)
  blocking collectives  120 us (20%)
  other arithmetic  29.7 us (5%)
  between operations  15.7 us (3%)
  local copies, waits for them, and re-layouts  15.4 us (3%)
    psum x1, waiting for transfers between devices, body(): lax.psum((gate_terms, up_terms, square_terms), 'req')  165 us
    unnamed x5, waiting for transfers between devices  109 us
    psum x1, waiting for transfers between devices, body(): projected = lax.psum(projected, 'exp')  107 us
    psum x1, blocking collectives, body(): lax.psum((gate_terms, up_terms, square_terms), 'req')  48.6 us
    all_gather x2, blocking collectives, merged_2(): gathered = jax.tree.map(lambda a: lax.all_gather(a, axis), part)  38.5 us
    all_gather x1, blocking collectives, body(): lax.all_gather(head_cols, 'req', axis=0, tiled=True)  32.4 us
    all_gather x1, waiting for transfers between devices, merged_2(): gathered = jax.tree.map(lambda a: lax.all_gather(a, axis), part)  31.6 us
    add x15, other arithmetic, combine_parts(): first_acc * first_scale[..., None] + second_acc * second_scale[..., None]  18.3 us
  transfers between devices with their start and end apart: 4, of which 4 were waited for; matrix products, arithmetic and copies ran while one was open for 1% of the time, Pallas kernels for 0%

commit v1 on v0

v1 whole, which is shorter than its diff:
```python
import functools

import jax
import jax.numpy as jnp
from jax import lax
from jax.experimental import pallas as pl
from jax.experimental.pallas import tpu as pltpu
from jax.sharding import PartitionSpec as P

MESH = pl.DeviceIdType.MESH
BF = jnp.bfloat16
F32 = jnp.float32

D = 4096
HD = 128
GROUPS = 4
NZ = 16
NE = 16
SLOTS = 256
TOKENS = 256
HALF = 768
WIDE = 2 * HALF + 128
NEG = -1e30
EPS = 1e-6
CENTERS = (-6, -3, 0, 3, 6)
FAR = (6, -6, 3, -3)


def remote(src, dst, send, recv, dev):
    return pltpu.make_async_remote_copy(
        src_ref=src, dst_ref=dst, send_sem=send, recv_sem=recv, device_id=dev, device_id_type=MESH
    )


def dot(a, b):
    return jnp.dot(a, b, preferred_element_type=F32)


def dot_t(a, b):
    return lax.dot_general(a, b, (((0,), (0,)), ((), ())), preferred_element_type=F32)


def dot_nt(a, b):
    return lax.dot_general(a, b, (((1,), (1,)), ((), ())), preferred_element_type=F32)


def hi_lo(v, rows):
    high = v.astype(BF).astype(F32)
    lane = lax.broadcasted_iota(jnp.int32, (rows, 128), 1)
    return jnp.where(lane < 64, high, v - high).astype(BF)


def from_hi_lo(block):
    return jnp.sum(block, axis=1, keepdims=True) * (1.0 / 64.0)


def kernel(
    len_ref, q_ref, nk_ref, nv_ref, kc_ref, vc_ref, op_ref, res_ref, gain_ref, gw_ref, uw_ref, dw_ref,
    ids_ref, rw_ref, o_ref,
    kc, vc, opw, resb, gainb, wg, wu, wd, resf,
    acc, stat, acc_in, stat_in, wt, attn, cs1, cr1, cs2, cr2,
    nb, hb, sel_in, sel_out, slot_w, part, from_left, from_right, from_far, s2, r2, own, act, mo, fr,
    loc, snd, rcv, bulk_s, bulk_r,
):
    r = lax.axis_index("req")
    e = lax.axis_index("exp")
    z = r // 2
    c = lax.rem(r, 2)
    oc = 1 - c
    ex = lax.rem(e, 4)
    ey = e // 4

    def at_z(off):
        return (2 * lax.rem(z + off + NZ, NZ) + c, e)

    sibling = (2 * z + oc, e)

    barrier = pltpu.get_barrier_semaphore()

    def greet(dev):
        pl.semaphore_signal(barrier, inc=1, device_id=dev, device_id_type=MESH)

    for off in (6, -6, 3, -3, 2, -2, 1, -1):
        greet(at_z(off))

    def greet_plane(i, carry):
        other = lax.rem(e + i, NE)
        greet((r, other))
        greet((2 * z + oc, other))
        return carry

    lax.fori_loop(1, NE, greet_plane, 0)
    greet(sibling)

    copies = []

    def fetch(src, dst):
        cp = pltpu.make_async_copy(src, dst, loc.at[len(copies)])
        cp.start()
        copies.append(cp)
        return cp

    cache_copies = []
    for s in range(2):
        cache_copies.append(fetch(kc_ref.at[s], kc.at[s]))
        cache_copies.append(fetch(vc_ref.at[s], vc.at[s]))
    mine = pl.multiple_of(c * HALF, 128)
    theirs = pl.multiple_of(oc * HALF, 128)
    early = [fetch(op_ref, opw.at[c]), fetch(res_ref, resb.at[c])]
    weights = [
        fetch(gw_ref.at[:, :, pl.ds(mine, HALF)], wg.at[:, c]),
        fetch(uw_ref.at[:, :, pl.ds(mine, HALF)], wu.at[:, c]),
        fetch(dw_ref.at[:, pl.ds(mine, HALF), :], wd.at[:, c]),
    ]
    gainb[c] = jnp.broadcast_to(gain_ref[...], (8, 128))

    lane = lax.broadcasted_iota(jnp.int32, (1, 128), 1)
    lane_slot = lax.rem(lane, 8) // 4
    lane_step = lax.rem(lane, 4)
    first = lane_slot == 0
    n0 = len_ref[2 * r]
    n1 = len_ref[2 * r + 1]
    count = jnp.where(first, n0, n1)
    place = lax.broadcasted_iota(jnp.int32, (384, 128), 0) * NE + e
    live = place < count
    fresh_row = lax.broadcasted_iota(jnp.int32, (16, 128), 0)
    fresh_live = (
        (fresh_row < 8)
        & (fresh_row // 4 == lane_slot)
        & (lax.rem(fresh_row, 4) <= lane_step)
        & (jnp.zeros((16, 128), jnp.int32) + e == 0)
    )
    zeros8 = jnp.zeros((8, 512), F32)
    fresh_k = jnp.concatenate([nk_ref[...].astype(F32), zeros8], axis=0).astype(BF)
    fresh_v = jnp.concatenate([nv_ref[...].astype(F32), zeros8], axis=0).astype(BF)
    scale = HD ** (-0.5)
    for cp in cache_copies:
        cp.wait()
    stat_row = lax.broadcasted_iota(jnp.int32, (8, 128), 0)
    for g in range(GROUPS):
        cols = slice(g * HD, (g + 1) * HD)
        q = jnp.concatenate(
            [q_ref[:, (g * 16 + j) * HD:(g * 16 + j + 1) * HD].astype(F32) for j in range(16)], axis=0
        ).astype(BF)
        s0 = dot_nt(kc[0, :, cols], q)
        s1 = dot_nt(kc[1, :, cols], q)
        score = jnp.where(live, jnp.where(first, s0, s1) * scale, NEG)
        fresh = jnp.where(fresh_live, dot_nt(fresh_k[:, cols], q) * scale, NEG)
        top = jnp.maximum(jnp.max(score, axis=0, keepdims=True), jnp.max(fresh, axis=0, keepdims=True))
        w = jnp.where(live, jnp.exp(score - top), 0.0)
        wf = jnp.where(fresh_live, jnp.exp(fresh - top), 0.0)
        total = jnp.sum(w, axis=0, keepdims=True) + jnp.sum(wf, axis=0, keepdims=True)
        w0 = jnp.where(first, w, 0.0).astype(BF)
        w1 = jnp.where(first, 0.0, w).astype(BF)
        mixed = dot_t(w0, vc[0, :, cols]) + dot_t(w1, vc[1, :, cols]) + dot_t(wf.astype(BF), fresh_v[:, cols])
        acc[g] = mixed.astype(BF)
        stat[g] = jnp.where(stat_row == 0, top, total)

    for cp in early:
        cp.wait()
    pl.semaphore_wait(barrier, 8 + 2 * (NE - 1) + 1)

    def acc_copy(i):
        other = lax.rem(e + i, NE)
        rows = pl.ds(pl.multiple_of(32 * lax.rem(other, 4), 32), 32)
        return (
            remote(acc.at[other // 4, rows], acc_in.at[e], bulk_s.at[0], bulk_r.at[0], (r, other)),
            remote(stat.at[other // 4], stat_in.at[e], bulk_s.at[1], bulk_r.at[1], (r, other)),
        )

    def acc_send(i, carry):
        for cp in acc_copy(i):
            cp.start()
        return carry

    lax.fori_loop(1, NE, acc_send, 0)

    sends = []

    def send(src, dst, dev):
        cp = remote(src, dst, snd.at[len(sends)], rcv.at[len(sends)], dev)
        cp.start()
        sends.append(cp)
        return cp

    opw_cp = send(op_ref, opw.at[c], sibling)
    res_cp = send(res_ref, resb.at[c], sibling)
    gain_cp = send(gainb.at[c], gainb.at[c], sibling)
    wg_cp = send(gw_ref.at[:, :, pl.ds(theirs, HALF)], wg.at[:, c], sibling)
    wu_cp = send(uw_ref.at[:, :, pl.ds(theirs, HALF)], wu.at[:, c], sibling)
    wd_cp = send(dw_ref.at[:, pl.ds(theirs, HALF), :], wd.at[:, c], sibling)

    acc_in[e] = acc[ey, pl.ds(pl.multiple_of(32 * ex, 32), 32)]
    stat_in[e] = stat[ey]

    ids = ids_ref[...]
    rw = rw_ref[...]
    col = lax.broadcasted_iota(jnp.int32, (256, 256), 1)
    row = lax.broadcasted_iota(jnp.int32, (256, 256), 0)
    upto = jnp.where(row <= col, 1.0, 0.0).astype(BF)
    real = (lax.rem(col, 128) // 8) * 16 + (col // 128) * 8 + lax.rem(col, 8)
    perm = jnp.where(row == real, 1.0, 0.0).astype(BF)
    row8 = lax.broadcasted_iota(jnp.int32, (8, 256), 0)
    hit0 = ids == 2 * e
    hit1 = ids == 2 * e + 1
    on0 = jnp.max(jnp.where(hit0, 1.0, 0.0), axis=0, keepdims=True)
    on1 = jnp.max(jnp.where(hit1, 1.0, 0.0), axis=0, keepdims=True)
    rw0 = jnp.sum(jnp.where(hit0, rw, 0.0), axis=0, keepdims=True)
    rw1 = jnp.sum(jnp.where(hit1, rw, 0.0), axis=0, keepdims=True)
    on = jnp.where(row8 == 0, on0, jnp.where(row8 == 1, on1, 0.0))
    rank = dot(on.astype(BF), upto)
    pos = jnp.where(on > 0.5, rank, 0.0)
    pos_perm = dot(pos.astype(BF), perm)
    slot_id = lax.broadcasted_iota(jnp.int32, (128, 256), 0).astype(F32) + 1.0
    chosen = []
    for k, weight in ((0, rw0), (1, rw1)):
        here = pl.ds(128 * k, 128)
        sel_in[here, :] = jnp.where(pos_perm[k:k + 1, :] == slot_id, 1.0, 0.0).astype(BF)
        pick = jnp.where(pos[k:k + 1, :] == slot_id, 1.0, 0.0)
        slot_w[here, :] = jnp.broadcast_to(jnp.sum(pick * weight, axis=1, keepdims=True), (128, 128))
        chosen.append(pick)
    sel_out[...] = jnp.transpose(jnp.concatenate(chosen, axis=0)).astype(BF)

    pltpu.make_async_copy(acc_in.at[pl.ds(0, NE - 1)], acc_in.at[pl.ds(0, NE - 1)], bulk_r.at[0]).wait()
    pltpu.make_async_copy(stat_in.at[pl.ds(0, NE - 1)], stat_in.at[pl.ds(0, NE - 1)], bulk_r.at[1]).wait()
    tops = stat_in[:, 0, :]
    totals = stat_in[:, 1, :]
    rel = jnp.exp(tops - jnp.max(tops, axis=0, keepdims=True))
    rel = rel / jnp.sum(rel * totals, axis=0, keepdims=True)
    wt[...] = jnp.transpose(jnp.concatenate([rel, jnp.zeros((112, 128), F32)], axis=0))
    shares = wt[pl.ds(pl.multiple_of(32 * ex, 32), 32), :]
    merged = shares[:, 0:1] * acc_in[0].astype(F32)
    for src in range(1, NE):
        merged = merged + shares[:, src:src + 1] * acc_in[src].astype(F32)
    attn[z] = merged.astype(BF)

    def gather(chunk):
        first_leg = {off: send(chunk(z), chunk(z), at_z(off)) for off in FAR}
        last_leg = [send(chunk(z), chunk(z), at_z(off)) for off in (1, -1)]
        for off in (3, -3, 6, -6):
            first_leg[off].wait_recv()
            src = lax.rem(z - off + NZ, NZ)
            for step in (1, -1):
                last_leg.append(send(chunk(src), chunk(src), at_z(step)))
        way = 1 - 2 * c
        src = lax.rem(z - 6 * way + NZ, NZ)
        last_leg.append(send(chunk(src), chunk(src), at_z(2 * way)))
        for cp in last_leg:
            cp.wait_recv()

    gather(lambda i: attn.at[i])

    opw_cp.wait_recv()
    res_cp.wait_recv()
    gain_cp.wait_recv()
    for k in range(2):
        blocks = resb[k].astype(F32).reshape(NZ, 2, 8, 128)
        resf[k] = jnp.where(c == 0, blocks[:, 0], blocks[:, 1]).reshape(128, 128)
    heads = attn[...].astype(F32).reshape(NZ, 4, 8, 128)
    x = jnp.concatenate([heads[:, j].reshape(128, 128) for j in range(4)], axis=1).astype(BF)

    def row_peer(k):
        return (r, ey * 4 + lax.rem(ex + k, 4))

    def column_peer(k):
        return (r, lax.rem(ey + k, 4) * 4 + ex)

    first_sum = []
    proj = []
    for k, peer in ((0, row_peer), (1, column_peer)):
        proj.append(dot(x, opw[k]))
        cs1[k] = proj[k].astype(BF)
        first_sum.append([send(cs1.at[k], cr1.at[k, i - 1], peer(i)) for i in (2, 1, 3)])
    second_sum = []
    for k, peer in ((0, column_peer), (1, row_peer)):
        for cp in first_sum[k]:
            cp.wait_recv()
        for i in range(3):
            proj[k] = proj[k] + cr1[k, i].astype(F32)
        cs2[k] = proj[k].astype(BF)
        second_sum.append([send(cs2.at[k], cr2.at[k, i - 1], peer(i)) for i in (2, 1, 3)])
    hidden = []
    square = jnp.zeros((128, 128), F32)
    mine_rows = pl.ds(pl.multiple_of(128 * c, 128), 128)
    for k in range(2):
        for cp in second_sum[k]:
            cp.wait_recv()
        h = proj[k] + resf[k]
        for i in range(3):
            h = h + cr2[k, i].astype(F32)
        hidden.append(h)
        square = square + h * h
        nb[mine_rows, 128 * k:128 * k + 128] = (h * gainb[k, 0:1, :]).astype(BF)
    nb[mine_rows, 256:384] = hi_lo(jnp.sum(square, axis=1, keepdims=True), 128)
    nb_cp = send(nb.at[mine_rows], nb.at[mine_rows], sibling)
    hb[c] = jnp.where(c == 0, hidden[0], hidden[1])
    hb[2] = jnp.where(c == 0, hidden[1], hidden[0])
    hb_cp = send(hb.at[2], hb.at[c], sibling)

    for cp in weights:
        cp.wait()
    wg_cp.wait_recv()
    wu_cp.wait_recv()
    nb_cp.wait_recv()
    rows_in = dot(sel_in[...], nb[...])
    part[:, 2 * HALF:] = hi_lo(from_hi_lo(rows_in[:, 256:384]), SLOTS)
    rows_in = rows_in[:, :256].astype(BF)
    for k in range(2):
        here = slice(128 * k, 128 * k + 128)
        part[here, 0:HALF] = dot(rows_in[here], wg[k].reshape(256, HALF)).astype(BF)
        part[here, HALF:2 * HALF] = dot(rows_in[here], wu[k].reshape(256, HALF)).astype(BF)

    def rows_of(i):
        return pl.ds(pl.multiple_of(16 * lax.rem(i + 2 * NZ, NZ), 16), 16)

    way = 1 - 2 * c
    far_cp = send(part.at[rows_of(z + 8)], from_far, at_z(-2 * way))
    left_cp = [None] * 5
    right_cp = [None] * 5
    for k in (0, 4, 1, 3, 2):
        left_cp[k] = send(part.at[rows_of(z + 1 - CENTERS[k])], from_left.at[k], at_z(1))
        right_cp[k] = send(part.at[rows_of(z - 1 - CENTERS[k])], from_right.at[k], at_z(-1))
    far_cp.wait_recv()
    second = [None] * 5
    for k in (0, 4, 1, 3, 2):
        left_cp[k].wait_recv()
        right_cp[k].wait_recv()
        s = part[rows_of(z - CENTERS[k]), :].astype(F32) + from_left[k].astype(F32) + from_right[k].astype(F32)
        if k == 0:
            s = s + jnp.where(c == 1, from_far[...].astype(F32), 0.0)
        if k == 4:
            s = s + jnp.where(c == 0, from_far[...].astype(F32), 0.0)
        if k == 2:
            own[...] = s
        else:
            s2[k, :, 0:2 * HALF] = s[:, 0:2 * HALF].astype(BF)
            s2[k, :, 2 * HALF:] = hi_lo(from_hi_lo(s[:, 2 * HALF:]), 16)
            second[k] = send(s2.at[k], r2.at[k], at_z(-CENTERS[k]))
    s = own[...]
    for k in (1, 3, 0, 4):
        second[k].wait_recv()
        s = s + r2[k].astype(F32)
    norm = lax.rsqrt(from_hi_lo(s[:, 2 * HALF:]) * (1.0 / D) + EPS)
    gate = norm * s[:, 0:HALF]
    up = norm * s[:, HALF:2 * HALF]
    act[rows_of(z), :] = (gate / (1.0 + jnp.exp(-gate)) * up).astype(BF)

    gather(lambda i: act.at[pl.ds(pl.multiple_of(16 * i, 16), 16)])

    wd_cp.wait_recv()
    for k in range(2):
        down = jnp.concatenate([dot(act[128 * x2:128 * x2 + 128, :], wd[x2, k]) for x2 in range(2)], axis=0)
        mo[k] = dot(sel_out[...], (down * slot_w[...]).astype(BF)).astype(BF)

    def rows_for(other):
        return pl.ds(pl.multiple_of(16 * other, 16), 16)

    def out_copy(i, core):
        other = lax.rem(e + i, NE)
        return remote(
            mo.at[core, rows_for(other)], fr.at[2 * e + c], bulk_s.at[2], bulk_r.at[2], (2 * z + core, other)
        )

    def out_send(i, carry):
        out_copy(i, c).start()
        out_copy(i, oc).start()
        return carry

    lax.fori_loop(1, NE, out_send, 0)
    out_copy(0, oc).start()
    fr[2 * e + c] = mo[c, rows_for(e)]
    hb_cp.wait_recv()
    first_rows = pl.ds(pl.multiple_of(8 * e, 8), 8)
    base = jnp.concatenate([hb[0, first_rows], hb[1, first_rows]], axis=0)
    pltpu.make_async_copy(fr.at[pl.ds(0, 2 * NE - 1)], fr.at[pl.ds(0, 2 * NE - 1)], bulk_r.at[2]).wait()
    o_ref[...] = (base + jnp.sum(fr[...].astype(F32), axis=0)).astype(BF)

    for cp in sends:
        cp.wait_send()
    pltpu.make_async_copy(acc_in.at[pl.ds(0, NE - 1)], acc_in.at[pl.ds(0, NE - 1)], bulk_s.at[0]).wait()
    pltpu.make_async_copy(stat_in.at[pl.ds(0, NE - 1)], stat_in.at[pl.ds(0, NE - 1)], bulk_s.at[1]).wait()
    pltpu.make_async_copy(fr.at[pl.ds(0, 2 * NE - 1)], fr.at[pl.ds(0, 2 * NE - 1)], bulk_s.at[2]).wait()


def layer(
    queries, new_keys, new_values, key_cache, value_cache, lengths, out_proj, residual, norm_gain,
    gate_weight, up_weight, down_weight, expert_ids, route_weights,
):
    vmem = pl.BlockSpec(memory_space=pltpu.VMEM)
    hbm = pl.BlockSpec(memory_space=pl.ANY)
    smem = pl.BlockSpec(memory_space=pltpu.SMEM)
    scratch = [
        ((2, 384, 512), BF), ((2, 384, 512), BF), ((2, 512, 128), BF), ((2, 256, 128), BF), ((2, 8, 128), F32),
        ((2, 2, 128, HALF), BF), ((2, 2, 128, HALF), BF), ((2, 2, HALF, 128), BF), ((2, 128, 128), F32),
        ((4, 128, 128), BF), ((4, 8, 128), F32), ((16, 32, 128), BF), ((16, 8, 128), F32), ((128, 128), F32),
        ((16, 32, 128), BF), ((2, 128, 128), BF), ((2, 3, 128, 128), BF), ((2, 128, 128), BF), ((2, 3, 128, 128), BF),
        ((256, 384), BF), ((3, 128, 128), F32), ((256, 256), BF), ((256, 256), BF), ((256, 128), F32),
        ((256, WIDE), BF), ((5, 16, WIDE), BF), ((5, 16, WIDE), BF), ((16, WIDE), BF),
        ((5, 16, WIDE), BF), ((5, 16, WIDE), BF), ((16, WIDE), F32), ((256, HALF), BF),
        ((2, 256, 128), BF), ((32, 16, 128), BF),
    ]
    sems = [16, 80, 80, 3, 3]
    return pl.pallas_call(
        kernel,
        name="layer",
        out_shape=jax.ShapeDtypeStruct((16, 128), BF),
        in_specs=[smem, vmem, vmem, vmem, hbm, hbm, hbm, hbm, vmem, hbm, hbm, hbm, vmem, vmem],
        out_specs=vmem,
        scratch_shapes=[pltpu.VMEM(s, t) for s, t in scratch] + [pltpu.SemaphoreType.DMA((n,)) for n in sems],
        compiler_params=pltpu.CompilerParams(
            collective_id=0, has_side_effects=True, vmem_limit_bytes=48 * 1024 * 1024
        ),
    )(
        lengths, queries, new_keys, new_values, key_cache[:, :, 0, :], value_cache[:, :, 0, :], out_proj, residual,
        norm_gain.reshape(1, 128), gate_weight, up_weight, down_weight, expert_ids.T, route_weights.T,
    )


def solution(mesh):
    in_specs = (
        P("req", None), P("req", None), P("req", None), P("req", None, "exp", None), P("req", None, "exp", None),
        P(), P("exp", "req"), P(None, "req"), P("req"), P("exp", "req", None), P("exp", "req", None),
        P("exp", None, "req"), P(), P(),
    )
    return jax.shard_map(layer, mesh=mesh, in_specs=in_specs, out_specs=P("exp", "req"), check_vma=False)
```

time: 602 us -> 94.8 us (0.16)
  waiting for transfers between devices: 413 us -> 0 us
  blocking collectives: 120 us -> 0 us
  Pallas kernels: 0 us -> 82.6 us
  other arithmetic: 29.7 us -> 0 us
  between operations: 15.7 us -> 0.03 us
    psum x2 -> x0, waiting for transfers between devices: 272 us -> none  [the longest x1 165 us: body(): lax.psum((gate_terms, up_terms, square_terms), 'req')]
    unnamed x5 -> x0, waiting for transfers between devices: 109 us -> none
    pallas_call x0 -> x1, Pallas kernels: none -> 82.6 us  [layer(): pl.pallas_call(kernel, name='layer', out_shape=jax.ShapeDtypeStruct((16,...]
    all_gather x3 -> x0, blocking collectives: 70.9 us -> none  [the longest x2 38.5 us: merged_2(): gathered = jax.tree.map(lambda a: lax.all_gather(a, axis), part)]
    psum x1 -> x0, blocking collectives: 48.6 us -> none  [body(): lax.psum((gate_terms, up_terms, square_terms), 'req')]
    all_gather x1 -> x0, waiting for transfers between devices: 31.6 us -> none  [merged_2(): gathered = jax.tree.map(lambda a: lax.all_gather(a, axis), part)]
    add x35 -> x0, other arithmetic: 19 us -> none  [the longest x15 18.3 us: combine_parts(): first_acc * first_scale[..., None] + second_acc * second_scale[..., None]]
    gather x8 -> x0, local copies, waits for them, and re-layouts: 9.16 us -> none  [the longest x2 2.53 us: body(): row_weights.append(jnp.where(filled, weight_row[chosen], 0.0))]
  transfers between devices with their start and end apart: 4 -> 0, of which waited for: 4 -> 0; matrix products, arithmetic and copies ran while one was open for 1% -> 0% of each run, Pallas kernels for 0% -> 0%
where the time goes in v1:
time: 94.8 us; the launch traced here: 94.3 us
  Pallas kernels  82.6 us (87%)
  local copies, waits for them, and re-layouts  11.7 us (12%)
    pallas_call x1, Pallas kernels, layer(): pl.pallas_call(kernel, name='layer', out_shape=jax.ShapeDtypeStruct((16,...  82.6 us
    unnamed x29, local copies, waits for them, and re-layouts  11.7 us

profile of v1, /device:TPU:1, one launch (start us, length us, event | category | flops | bytes accessed | tf_op | source)
XLA Modules:
  0.0 94.3 jit_solution(4373425240771324140)
XLA Ops:
  0.0 0.0 copy-start.8
  0.0 0.0 copy-start.12
  0.0 0.0 copy-start.13
  0.0 0.7 copy-done.8
  0.7 0.0 copy-done.12
  0.7 0.0 copy-done.13
  0.7 0.0 copy-start
  0.7 1.1 %copy-done = bf16[2,384,1,512]{3,1,2,0:T(8,128)(2,1)S(1)} copy-done((bf16[2,384,1,512]{3,1,2,0:T(8,128)(2,1)S(1)}, bf16[2,384,1,512]{3,1,2,0:T(8,128)(2,1)}, u32[]{:S(2)}) %copy-start) | copy-done | bytes 786456
  1.8 0.0 copy-start.1
  1.8 1.1 %copy-done.1 = bf16[2,384,1,512]{3,1,2,0:T(8,128)(2,1)S(1)} copy-done((bf16[2,384,1,512]{3,1,2,0:T(8,128)(2,1)S(1)}, bf16[2,384,1,512]{3,1,2,0:T(8,128)(2,1)}, u32[]{:S(2)}) %copy-start.1) | copy-done | bytes 786456
  3.0 0.0 copy-start.2
  3.0 1.1 %copy-done.2 = bf16[2,128,1536]{2,1,0:T(8,128)(2,1)S(1)} copy-done((bf16[2,128,1536]{2,1,0:T(8,128)(2,1)S(1)}, bf16[2,128,1536]{2,1,0:T(8,128)(2,1)}, u32[]{:S(2)}) %copy-start.2) | copy-done | bytes 786456
  4.1 0.0 copy-start.3
  4.1 1.1 %copy-done.3 = bf16[2,128,1536]{2,1,0:T(8,128)(2,1)S(1)} copy-done((bf16[2,128,1536]{2,1,0:T(8,128)(2,1)S(1)}, bf16[2,128,1536]{2,1,0:T(8,128)(2,1)}, u32[]{:S(2)}) %copy-start.3) | copy-done | bytes 786456
  5.2 0.0 copy-start.4
  5.2 1.1 %copy-done.4 = bf16[2,1536,128]{2,1,0:T(8,128)(2,1)S(1)} copy-done((bf16[2,1536,128]{2,1,0:T(8,128)(2,1)S(1)}, bf16[2,1536,128]{2,1,0:T(8,128)(2,1)}, u32[]{:S(2)}) %copy-start.4) | copy-done | bytes 786456
  6.4 0.0 copy-start.5
  6.4 0.9 copy-done.5
  7.3 0.0 copy-start.6
  7.3 0.9 copy-done.6
  8.2 0.0 copy-start.7
  8.2 0.8 copy-done.7
  9.0 0.0 copy-start.9
  9.0 0.7 copy-done.9
  9.7 0.0 copy-start.10
  9.7 0.7 copy-done.10
  10.4 0.0 copy-start.11
  10.4 0.7 copy-done.11
  11.1 82.6 %layer.1 = bf16[16,128]{1,0:T(8,128)(2,1)S(1)} custom-call(s32[64]{0:T(128)S(1)} %copy-done.12, bf16[8,8192]{1,0:T(8,128)(2,1)S(1)} %copy-done.5, bf16[8,512]{1,0:T(8,128)(2,1)S(1)} %copy-done.8, bf16[8,512]{1,0:T(8,128)(2,1)S(1)} %copy-done.9, bf16[2,384,512]{2,1,0:T(8,128)(2,1)S(1)} %bitcast.5, bf16[2,384,512]{2,1,0:T(8,128)(2,1)S(1)} %bitcast.6, ...), custom_call_target="tpu_custom_call" | custom-call | tf_op jit(solution)/shard_map/layer/pallas_call | solution.py:403
  93.7 0.6 copy.16
Async XLA Ops:
  0.0 0.7 copy-start.8
  0.0 0.7 copy-start.12
  0.0 0.7 copy-start.13
  0.7 1.1 %copy-start = (bf16[2,384,1,512]{3,1,2,0:T(8,128)(2,1)S(1)}, bf16[2,384,1,512]{3,1,2,0:T(8,128)(2,1)}, u32[]{:S(2)}) copy-start(bf16[2,384,1,512]{3,1,2,0:T(8,128)(2,1)} %param.17) | copy-start | bytes 2359300
  1.8 1.1 %copy-start.1 = (bf16[2,384,1,512]{3,1,2,0:T(8,128)(2,1)S(1)}, bf16[2,384,1,512]{3,1,2,0:T(8,128)(2,1)}, u32[]{:S(2)}) copy-start(bf16[2,384,1,512]{3,1,2,0:T(8,128)(2,1)} %param.18) | copy-start | bytes 2359300
  3.0 1.1 %copy-start.2 = (bf16[2,128,1536]{2,1,0:T(8,128)(2,1)S(1)}, bf16[2,128,1536]{2,1,0:T(8,128)(2,1)}, u32[]{:S(2)}) copy-start(bf16[2,128,1536]{2,1,0:T(8,128)(2,1)} %gw_ref.1) | copy-start | bytes 2359300
  4.1 1.1 %copy-start.3 = (bf16[2,128,1536]{2,1,0:T(8,128)(2,1)S(1)}, bf16[2,128,1536]{2,1,0:T(8,128)(2,1)}, u32[]{:S(2)}) copy-start(bf16[2,128,1536]{2,1,0:T(8,128)(2,1)} %uw_ref.1) | copy-start | bytes 2359300
  5.2 1.1 %copy-start.4 = (bf16[2,1536,128]{2,1,0:T(8,128)(2,1)S(1)}, bf16[2,1536,128]{2,1,0:T(8,128)(2,1)}, u32[]{:S(2)}) copy-start(bf16[2,1536,128]{2,1,0:T(8,128)(2,1)} %dw_ref.1) | copy-start | bytes 2359300
  6.4 0.9 copy-start.5
  7.3 0.9 copy-start.6
  8.2 0.8 copy-start.7
  9.0 0.7 copy-start.9
  9.7 0.7 copy-start.10
  10.4 0.7 copy-start.11

commit v2 on v1

v2 whole, which is shorter than its diff:
```python
import functools

import jax
import jax.numpy as jnp
from jax import lax
from jax.experimental import pallas as pl
from jax.experimental.pallas import tpu as pltpu
from jax.sharding import PartitionSpec as P

MESH = pl.DeviceIdType.MESH
BF = jnp.bfloat16
F32 = jnp.float32

D = 4096
HD = 128
GROUPS = 4
NZ = 16
NE = 16
SLOTS = 256
TOKENS = 256
HALF = 768
QUART = HALF // 2
WIDE = 2 * HALF + 128
GATE = (slice(0, QUART), slice(WIDE - 2 * QUART, WIDE - QUART))
UP = (slice(QUART, 2 * QUART), slice(WIDE - QUART, WIDE))
SQ = slice(2 * QUART, 2 * QUART + 128)
PIECE = (slice(0, 2 * QUART + 128), slice(2 * QUART + 128, WIDE))
NEG = -1e30
EPS = 1e-6
CENTERS = (-6, -3, 0, 3, 6)
FAR = (6, -6, 3, -3)
PLANE = sorted(
    ((dy, dx) for dy in range(4) for dx in range(4) if dy or dx), key=lambda s: -sum(min(v, 4 - v) for v in s)
)


def remote(src, dst, send, recv, dev):
    return pltpu.make_async_remote_copy(
        src_ref=src, dst_ref=dst, send_sem=send, recv_sem=recv, device_id=dev, device_id_type=MESH
    )


def dot(a, b):
    return jnp.dot(a, b, preferred_element_type=F32)


def dot_t(a, b):
    return lax.dot_general(a, b, (((0,), (0,)), ((), ())), preferred_element_type=F32)


def dot_nt(a, b):
    return lax.dot_general(a, b, (((1,), (1,)), ((), ())), preferred_element_type=F32)


def hi_lo(v, rows):
    high = v.astype(BF).astype(F32)
    lane = lax.broadcasted_iota(jnp.int32, (rows, 128), 1)
    return jnp.where(lane < 64, high, v - high).astype(BF)


def split3(v):
    high = v.astype(BF).astype(F32)
    mid = (v - high).astype(BF).astype(F32)
    return [high, mid, v - high - mid]


def from_hi_lo(block):
    return jnp.sum(block, axis=1, keepdims=True) * (1.0 / 64.0)


def kernel(
    len_hbm, q_hbm, nk_hbm, nv_hbm, kc_ref, vc_ref, op_ref, res_ref, gain_hbm, gw_ref, uw_ref, dw_ref,
    ids_hbm, rw_hbm, o_ref,
    len_ref, q_ref, nk_ref, nv_ref, gain_ref, ids_ref, rw_ref,
    kc, vc, opw, resb, gainb, wg, wu, wd, resf,
    acc, acc_in, wt, attn, cs1, cr1, cs2, cr2,
    nb, hid, sel_in, sel_out, slot_w, part, from_left, from_right, from_far, s2, r2, act, mo, fr,
    loc, snd, rcv, bulk_s, bulk_r, far_ready,
):
    r = lax.axis_index("req")
    e = lax.axis_index("exp")
    z = r // 2
    c = lax.rem(r, 2)
    oc = 1 - c
    ex = lax.rem(e, 4)
    ey = e // 4

    def at_z(off):
        return (2 * lax.rem(z + off + NZ, NZ) + c, e)

    sibling = (2 * z + oc, e)

    barrier = pltpu.get_barrier_semaphore()

    def greet(dev):
        pl.semaphore_signal(barrier, inc=1, device_id=dev, device_id_type=MESH)

    def plane(step):
        return lax.rem(ey + step[0], 4) * 4 + lax.rem(ex + step[1], 4)

    for step in PLANE:
        greet((r, plane(step)))
    for off in (3, -3, 2, -2, 1, -1):
        greet(at_z(off))
    greet(sibling)

    copies = []

    def fetch(src, dst):
        cp = pltpu.make_async_copy(src, dst, loc.at[len(copies)])
        cp.start()
        copies.append(cp)
        return cp

    cache_copies = [
        fetch(len_hbm, len_ref), fetch(q_hbm, q_ref), fetch(nk_hbm, nk_ref), fetch(nv_hbm, nv_ref),
    ]
    for s in range(2):
        cache_copies.append(fetch(kc_ref.at[s], kc.at[s]))
        cache_copies.append(fetch(vc_ref.at[s], vc.at[s]))
    mine = pl.multiple_of(c * HALF, 128)
    theirs = pl.multiple_of(oc * HALF, 128)
    early = [
        fetch(gain_hbm, gain_ref), fetch(ids_hbm, ids_ref), fetch(rw_hbm, rw_ref),
        fetch(op_ref, opw.at[c]), fetch(res_ref, resb.at[c]),
    ]
    weights = [
        fetch(gw_ref.at[:, :, pl.ds(mine, HALF)], wg.at[:, c]),
        fetch(uw_ref.at[:, :, pl.ds(mine, HALF)], wu.at[:, c]),
        fetch(dw_ref.at[:, pl.ds(mine, HALF), :], wd.at[:, c]),
    ]
    lane = lax.broadcasted_iota(jnp.int32, (1, 128), 1)
    lane_slot = lax.rem(lane, 8) // 4
    lane_step = lax.rem(lane, 4)
    first = lane_slot == 0
    for cp in cache_copies:
        cp.wait()
    n0 = len_ref[2 * r]
    n1 = len_ref[2 * r + 1]
    count = jnp.where(first, n0, n1)
    place = lax.broadcasted_iota(jnp.int32, (384, 128), 0) * NE + e
    live = place < count
    fresh_row = lax.broadcasted_iota(jnp.int32, (16, 128), 0)
    fresh_live = (
        (fresh_row < 8)
        & (fresh_row // 4 == lane_slot)
        & (lax.rem(fresh_row, 4) <= lane_step)
        & (jnp.zeros((16, 128), jnp.int32) + e == 0)
    )
    zeros8 = jnp.zeros((8, 512), F32)
    fresh_k = jnp.concatenate([nk_ref[...].astype(F32), zeros8], axis=0).astype(BF)
    fresh_v = jnp.concatenate([nv_ref[...].astype(F32), zeros8], axis=0).astype(BF)
    scale = HD ** (-0.5)
    for g in range(GROUPS):
        cols = slice(g * HD, (g + 1) * HD)
        q = jnp.concatenate(
            [q_ref[:, (g * 16 + j) * HD:(g * 16 + j + 1) * HD].astype(F32) for j in range(16)], axis=0
        ).astype(BF)
        s0 = dot_nt(kc[0, :, cols], q)
        s1 = dot_nt(kc[1, :, cols], q)
        score = jnp.where(live, jnp.where(first, s0, s1) * scale, NEG)
        fresh = jnp.where(fresh_live, dot_nt(fresh_k[:, cols], q) * scale, NEG)
        top = jnp.maximum(jnp.max(score, axis=0, keepdims=True), jnp.max(fresh, axis=0, keepdims=True))
        w = jnp.where(live, jnp.exp(score - top), 0.0)
        wf = jnp.where(fresh_live, jnp.exp(fresh - top), 0.0)
        total = jnp.sum(w, axis=0, keepdims=True) + jnp.sum(wf, axis=0, keepdims=True)
        w0 = jnp.where(first, w, 0.0).astype(BF)
        w1 = jnp.where(first, 0.0, w).astype(BF)
        mixed = dot_t(w0, vc[0, :, cols]) + dot_t(w1, vc[1, :, cols]) + dot_t(wf.astype(BF), fresh_v[:, cols])
        stats = jnp.concatenate(split3(top) + split3(total) + [jnp.zeros((10, 128), F32)], axis=0).astype(BF)
        mixed = mixed.astype(BF)
        for i in range(4):
            acc[4 * g + i, 0:32] = mixed[32 * i:32 * i + 32]
            acc[4 * g + i, 32:48] = stats

    for cp in early:
        cp.wait()
    gainb[c] = jnp.broadcast_to(gain_ref[...], (8, 128))
    pl.semaphore_wait(barrier, NE - 1 + 6 + 1)

    for step in PLANE:
        other = plane(step)
        remote(acc.at[other], acc_in.at[e], bulk_s.at[0], bulk_r.at[0], (r, other)).start()

    for off in (3, -3):
        pl.semaphore_signal(far_ready, inc=1, device_id=at_z(off), device_id_type=MESH)

    sends = []

    def send(src, dst, dev):
        cp = remote(src, dst, snd.at[len(sends)], rcv.at[len(sends)], dev)
        cp.start()
        sends.append(cp)
        return cp

    opw_cp = send(op_ref, opw.at[c], sibling)
    res_cp = send(res_ref, resb.at[c], sibling)
    gain_cp = send(gainb.at[c], gainb.at[c], sibling)
    wg_cp = send(gw_ref.at[:, :, pl.ds(theirs, HALF)], wg.at[:, c], sibling)
    wu_cp = send(uw_ref.at[:, :, pl.ds(theirs, HALF)], wu.at[:, c], sibling)
    wd_cp = send(dw_ref.at[:, pl.ds(theirs, HALF), :], wd.at[:, c], sibling)

    acc_in[e] = acc[e]

    ids = ids_ref[...]
    rw = rw_ref[...]
    col = lax.broadcasted_iota(jnp.int32, (256, 256), 1)
    row = lax.broadcasted_iota(jnp.int32, (256, 256), 0)
    upto = jnp.where(row <= col, 1.0, 0.0).astype(BF)
    real = (lax.rem(col, 128) // 8) * 16 + (col // 128) * 8 + lax.rem(col, 8)
    perm = jnp.where(row == real, 1.0, 0.0).astype(BF)
    row8 = lax.broadcasted_iota(jnp.int32, (8, 256), 0)
    hit0 = ids == 2 * e
    hit1 = ids == 2 * e + 1
    on0 = jnp.max(jnp.where(hit0, 1.0, 0.0), axis=0, keepdims=True)
    on1 = jnp.max(jnp.where(hit1, 1.0, 0.0), axis=0, keepdims=True)
    rw0 = jnp.sum(jnp.where(hit0, rw, 0.0), axis=0, keepdims=True)
    rw1 = jnp.sum(jnp.where(hit1, rw, 0.0), axis=0, keepdims=True)
    on = jnp.where(row8 == 0, on0, jnp.where(row8 == 1, on1, 0.0))
    rank = dot(on.astype(BF), upto)
    pos = jnp.where(on > 0.5, rank, 0.0)
    pos_perm = dot(pos.astype(BF), perm)
    slot_id = lax.broadcasted_iota(jnp.int32, (128, 256), 0).astype(F32) + 1.0
    chosen = []
    for k, weight in ((0, rw0), (1, rw1)):
        here = pl.ds(128 * k, 128)
        sel_in[here, :] = jnp.where(pos_perm[k:k + 1, :] == slot_id, 1.0, 0.0).astype(BF)
        pick = jnp.where(pos[k:k + 1, :] == slot_id, 1.0, 0.0)
        slot_w[here, :] = jnp.broadcast_to(jnp.sum(pick * weight, axis=1, keepdims=True), (128, 128))
        chosen.append(pick)
    sel_out[...] = jnp.transpose(jnp.concatenate(chosen, axis=0)).astype(BF)

    pltpu.make_async_copy(acc_in.at[pl.ds(0, NE - 1)], acc_in.at[pl.ds(0, NE - 1)], bulk_r.at[0]).wait()
    stats = acc_in[:, 32:48, :].astype(F32)
    tops = stats[:, 0] + stats[:, 1] + stats[:, 2]
    totals = stats[:, 3] + stats[:, 4] + stats[:, 5]
    rel = jnp.exp(tops - jnp.max(tops, axis=0, keepdims=True))
    rel = rel / jnp.sum(rel * totals, axis=0, keepdims=True)
    wt[...] = jnp.transpose(jnp.concatenate([rel, jnp.zeros((112, 128), F32)], axis=0))
    shares = wt[pl.ds(pl.multiple_of(32 * ex, 32), 32), :]
    merged = shares[:, 0:1] * acc_in[0, 0:32].astype(F32)
    for src in range(1, NE):
        merged = merged + shares[:, src:src + 1] * acc_in[src, 0:32].astype(F32)
    attn[z] = merged.astype(BF)

    way = 1 - 2 * c

    def near(i):
        return lax.rem(i + 2 * NZ, NZ)

    class Gather:
        def __init__(self, chunk):
            self.chunk = chunk
            self.first_leg = {off: self.pass_on(0, off) for off in FAR}
            self.last_leg = [self.pass_on(0, off) for off in (1, -1)]

        def pass_on(self, off, step):
            block = self.chunk(near(z - off))
            return send(block, block, at_z(step))

        def forward(self):
            for off in (3, -3, 6, -6):
                self.first_leg[off].wait_recv()
                self.last_leg += [self.pass_on(off, step) for step in (1, -1)]
            self.last_leg.append(self.pass_on(6 * way, 2 * way))

        def finish(self):
            for cp in self.last_leg:
                cp.wait_recv()

    def gather(chunks):
        parts = [Gather(chunk) for chunk in chunks]
        for p in parts:
            p.forward()
        for p in parts:
            p.finish()

    pl.semaphore_wait(far_ready, 2)
    gather([lambda i: attn.at[i]])

    opw_cp.wait_recv()
    res_cp.wait_recv()
    gain_cp.wait_recv()
    for k in range(2):
        blocks = resb[k].astype(F32).reshape(NZ, 2, 8, 128)
        for t in range(2):
            resf[t, k] = blocks[:, t].reshape(128, 128)
    heads = attn[...].astype(F32).reshape(NZ, 4, 8, 128)
    x = jnp.concatenate([heads[:, j].reshape(128, 128) for j in range(4)], axis=1).astype(BF)

    def row_peer(i, row=r):
        return (row, ey * 4 + lax.rem(ex + i, 4))

    def column_peer(i, row=r):
        return (row, lax.rem(ey + i, 4) * 4 + ex)

    first_sum = []
    proj = []
    for k, peer in ((0, row_peer), (1, column_peer)):
        proj.append(dot(x, opw[k]))
        cs1[k] = proj[k].astype(BF)
        first_sum.append([send(cs1.at[k], cr1.at[k, i - 1], peer(i)) for i in (2, 1, 3)])
    second_sum = []
    for k, peer in ((0, column_peer), (1, row_peer)):
        for cp in first_sum[k]:
            cp.wait_recv()
        for i in range(3):
            proj[k] = proj[k] + cr1[k, i].astype(F32)
        cs2[k] = proj[k].astype(BF)
        legs = [send(cs2.at[k], cr2.at[c, k, i], peer(i)) for i in (2, 1, 3)]
        second_sum.append(legs)
    square = jnp.zeros((128, 128), F32)
    mine_rows = pl.ds(pl.multiple_of(128 * c, 128), 128)
    for k in range(2):
        for cp in second_sum[k]:
            cp.wait_recv()
        h = proj[k] + resf[c, k]
        for i in range(1, 4):
            h = h + cr2[c, k, i].astype(F32)
        hid[c, k] = h
        square = square + h * h
        nb[mine_rows, 128 * k:128 * k + 128] = (h * gainb[k, 0:1, :]).astype(BF)
    nb[mine_rows, 256:384] = hi_lo(jnp.sum(square, axis=1, keepdims=True), 128)
    nb_cp = send(nb.at[mine_rows], nb.at[mine_rows], sibling)
    hid_cp = send(hid.at[c, oc], hid.at[c, oc], sibling)

    for cp in weights:
        cp.wait()
    wg_cp.wait_recv()
    wu_cp.wait_recv()
    nb_cp.wait_recv()
    rows_in = dot(sel_in[...], nb[...])
    part[:, SQ] = hi_lo(from_hi_lo(rows_in[:, 256:384]), SLOTS)
    rows_in = rows_in[:, :256].astype(BF)
    for h in range(2):
        units = slice(QUART * h, QUART * h + QUART)
        for k in range(2):
            here = slice(128 * k, 128 * k + 128)
            part[here, GATE[h]] = dot(rows_in[here], wg[k, :, :, units].reshape(256, QUART)).astype(BF)
            part[here, UP[h]] = dot(rows_in[here], wu[k, :, :, units].reshape(256, QUART)).astype(BF)

    def rows_of(i):
        return pl.ds(pl.multiple_of(16 * near(i), 16), 16)

    far_cp = [None] * 2
    left_cp = {}
    right_cp = {}

    def collect(h, k):
        left_cp[h, k] = send(part.at[rows_of(z + 1 - CENTERS[k]), PIECE[h]], from_left.at[k, :, PIECE[h]], at_z(1))
        right_cp[h, k] = send(part.at[rows_of(z - 1 - CENTERS[k]), PIECE[h]], from_right.at[k, :, PIECE[h]], at_z(-1))

    for h in range(2):
        far_cp[h] = send(part.at[rows_of(z + 8), PIECE[h]], from_far.at[:, PIECE[h]], at_z(-2 * way))
        for k in (0, 4):
            collect(h, k)
    for h in range(2):
        for k in (1, 3):
            collect(h, k)

    def collected(h, k):
        left_cp[h, k].wait_recv()
        right_cp[h, k].wait_recv()
        rows = rows_of(z - CENTERS[k])
        return (
            part[rows, PIECE[h]].astype(F32)
            + from_left[k, :, PIECE[h]].astype(F32)
            + from_right[k, :, PIECE[h]].astype(F32)
        )

    hops = {}

    def pass_on(h, k, s, off):
        if h == 0:
            s2[k, :, 0:2 * QUART] = s[:, 0:2 * QUART].astype(BF)
            s2[k, :, SQ] = hi_lo(from_hi_lo(s[:, SQ]), 16)
        else:
            s2[k, :, PIECE[h]] = s.astype(BF)
        hops[h, k] = send(s2.at[k, :, PIECE[h]], r2.at[k, :, PIECE[h]], at_z(off))

    for h in range(2):
        far_cp[h].wait_recv()
        for k, core, off in ((0, 1, 3), (4, 0, -3)):
            far = jnp.where(c == core, from_far[:, PIECE[h]].astype(F32), 0.0)
            pass_on(h, k, collected(h, k) + far, off)
    for h in range(2):
        collect(h, 2)
    for h in range(2):
        for k, before, off in ((1, 0, 3), (3, 4, -3)):
            s = collected(h, k)
            hops[h, before].wait_recv()
            pass_on(h, k, s + r2[before, :, PIECE[h]].astype(F32), off)
    gathers = []
    for h in range(2):
        s = collected(h, 2)
        for k in (1, 3):
            hops[h, k].wait_recv()
            s = s + r2[k, :, PIECE[h]].astype(F32)
        if h == 0:
            norm = lax.rsqrt(from_hi_lo(s[:, SQ]) * (1.0 / D) + EPS)
        gate = norm * s[:, 0:QUART]
        up = norm * s[:, QUART:2 * QUART]
        units = slice(QUART * h, QUART * h + QUART)
        act[rows_of(z), units] = (gate / (1.0 + jnp.exp(-gate)) * up).astype(BF)
        gathers.append(Gather(lambda i, units=units: act.at[rows_of(i), units]))
    for p in gathers:
        p.forward()
    for p in gathers:
        p.finish()

    wd_cp.wait_recv()
    for k in range(2):
        down = jnp.concatenate([dot(act[128 * x2:128 * x2 + 128, :], wd[x2, k]) for x2 in range(2)], axis=0)
        mo[k] = dot(sel_out[...], (down * slot_w[...]).astype(BF)).astype(BF)

    def rows_for(other):
        return pl.ds(pl.multiple_of(16 * other, 16), 16)

    def out_send(other, core):
        remote(
            mo.at[core, rows_for(other)], fr.at[2 * e + c], bulk_s.at[1], bulk_r.at[1], (2 * z + core, other)
        ).start()

    for step in PLANE:
        for core in (c, oc):
            out_send(plane(step), core)
    out_send(e, oc)
    fr[2 * e + c] = mo[c, rows_for(e)]
    first_rows = pl.ds(pl.multiple_of(8 * e, 8), 8)
    hid_cp.wait_recv()
    base = jnp.concatenate([hid[0, c, first_rows], hid[1, c, first_rows]], axis=0)
    pltpu.make_async_copy(fr.at[pl.ds(0, 2 * NE - 1)], fr.at[pl.ds(0, 2 * NE - 1)], bulk_r.at[1]).wait()
    o_ref[...] = (base + jnp.sum(fr[...].astype(F32), axis=0)).astype(BF)

    for cp in sends:
        cp.wait_send()
    pltpu.make_async_copy(acc_in.at[pl.ds(0, NE - 1)], acc_in.at[pl.ds(0, NE - 1)], bulk_s.at[0]).wait()
    pltpu.make_async_copy(fr.at[pl.ds(0, 2 * NE - 1)], fr.at[pl.ds(0, 2 * NE - 1)], bulk_s.at[1]).wait()


def layer(
    queries, new_keys, new_values, key_cache, value_cache, lengths, out_proj, residual, norm_gain,
    gate_weight, up_weight, down_weight, expert_ids, route_weights,
):
    vmem = pl.BlockSpec(memory_space=pltpu.VMEM)
    hbm = pl.BlockSpec(memory_space=pltpu.HBM)
    scratch = [
        ((8, 8192), BF), ((8, 512), BF), ((8, 512), BF), ((1, 128), F32), ((8, 256), jnp.int32), ((8, 256), F32),
        ((2, 384, 512), BF), ((2, 384, 512), BF), ((2, 512, 128), BF), ((2, 256, 128), BF), ((2, 8, 128), F32),
        ((2, 2, 128, HALF), BF), ((2, 2, 128, HALF), BF), ((2, 2, HALF, 128), BF), ((2, 2, 128, 128), F32),
        ((16, 48, 128), BF), ((16, 48, 128), BF), ((128, 128), F32),
        ((16, 32, 128), BF), ((2, 128, 128), BF), ((2, 3, 128, 128), BF), ((2, 128, 128), BF),
        ((2, 2, 4, 128, 128), BF), ((256, 384), BF), ((2, 2, 128, 128), F32), ((256, 256), BF), ((256, 256), BF), ((256, 128), F32),
        ((256, WIDE), BF), ((5, 16, WIDE), BF), ((5, 16, WIDE), BF), ((16, WIDE), BF),
        ((5, 16, WIDE), BF), ((5, 16, WIDE), BF), ((256, HALF), BF),
        ((2, 256, 128), BF), ((32, 16, 128), BF),
    ]
    sems = [16, 112, 112, 2, 2]
    return pl.pallas_call(
        kernel,
        name="layer",
        out_shape=jax.ShapeDtypeStruct((16, 128), BF),
        in_specs=[hbm] * 14,
        out_specs=vmem,
        scratch_shapes=[pltpu.SMEM((64,), jnp.int32)] + [pltpu.VMEM(s, t) for s, t in scratch] + [pltpu.SemaphoreType.DMA((n,)) for n in sems] + [pltpu.SemaphoreType.REGULAR],
        compiler_params=pltpu.CompilerParams(
            collective_id=0, has_side_effects=True, vmem_limit_bytes=64 * 1024 * 1024
        ),
    )(
        lengths, queries, new_keys, new_values, key_cache[:, :, 0, :], value_cache[:, :, 0, :], out_proj, residual,
        norm_gain.reshape(1, 128), gate_weight, up_weight, down_weight, expert_ids.T, route_weights.T,
    )


def solution(mesh):
    in_specs = (
        P("req", None), P("req", None), P("req", None), P("req", None, "exp", None), P("req", None, "exp", None),
        P(), P("exp", "req"), P(None, "req"), P("req"), P("exp", "req", None), P("exp", "req", None),
        P("exp", None, "req"), P(), P(),
    )
    return jax.shard_map(layer, mesh=mesh, in_specs=in_specs, out_specs=P("exp", "req"), check_vma=False)
```

time: 94.8 us -> 78.8 us (0.83)
  local copies, waits for them, and re-layouts: 11.7 us -> 1.28 us
  Pallas kernels: 82.6 us -> 77.4 us
    unnamed x29 -> x1, local copies, waits for them, and re-layouts: 11.7 us -> 1.28 us
    pallas_call x1, Pallas kernels: 82.6 us -> 77.4 us  [layer(): pl.pallas_call(kernel, name='layer', out_shape=jax.ShapeDtypeStruct((16,...]
where the time goes in v2:
time: 78.8 us; the launch traced here: 78.7 us
  Pallas kernels  77.4 us (98%)
  local copies, waits for them, and re-layouts  1.28 us (2%)
    pallas_call x1, Pallas kernels, layer(): pl.pallas_call(kernel, name='layer', out_shape=jax.ShapeDtypeStruct((16,...  77.4 us

profile of v2, /device:TPU:1, one launch (start us, length us, event | category | flops | bytes accessed | tf_op | source)
XLA Modules:
  0.0 78.7 jit_solution(14880469516534681992)
XLA Ops:
  0.0 77.4 %layer.1 = bf16[16,128]{1,0:T(8,128)(2,1)} custom-call(s32[64]{0:T(128)} %len_hbm.1, bf16[8,8192]{1,0:T(8,128)(2,1)} %q_hbm.1, bf16[8,512]{1,0:T(8,128)(2,1)} %nk_hbm.1, bf16[8,512]{1,0:T(8,128)(2,1)} %nv_hbm.1, bf16[2,384,512]{2,1,0:T(8,128)(2,1)} %bitcast.5, bf16[2,384,512]{2,1,0:T(8,128)(2,1)} %bitcast.6, bf16[512,128]{1,0:T(8,128)(2,1)} %op_ref.1, ...), custom_call_target="tpu_custom_call" | custom-call | tf_op jit(solution)/shard_map/layer/pallas_call | solution.py:459
  77.4 1.3 %copy.16 = bf16[16,128]{1,0:T(8,128)(2,1)} copy(bf16[16,128]{1,0:T(8,128)(2,1)} %layer.1) | data formatting | bytes 8192

commit v3 on v2

--- a/solution.py
+++ b/solution.py
@@ -29,6 +29,7 @@
 EPS = 1e-6
 CENTERS = (-6, -3, 0, 3, 6)
 FAR = (6, -6, 3, -3)
+COLUMN = (8, 7, -7, 6, -6, 5, -5, 4, -4, 3, -3, 2, -2, 1, -1)
 PLANE = sorted(
     ((dy, dx) for dy in range(4) for dx in range(4) if dy or dx), key=lambda s: -sum(min(v, 4 - v) for v in s)
 )
@@ -100,7 +101,7 @@
 
     for step in PLANE:
         greet((r, plane(step)))
-    for off in (3, -3, 2, -2, 1, -1):
+    for off in (4, -4, 3, -3, 2, -2, 1, -1):
         greet(at_z(off))
     greet(sibling)
 
@@ -176,13 +177,13 @@
     for cp in early:
         cp.wait()
     gainb[c] = jnp.broadcast_to(gain_ref[...], (8, 128))
-    pl.semaphore_wait(barrier, NE - 1 + 6 + 1)
+    pl.semaphore_wait(barrier, NE - 1 + 8 + 1)
 
     for step in PLANE:
         other = plane(step)
         remote(acc.at[other], acc_in.at[e], bulk_s.at[0], bulk_r.at[0], (r, other)).start()
 
-    for off in (3, -3):
+    for off in (4, -4):
         pl.semaphore_signal(far_ready, inc=1, device_id=at_z(off), device_id_type=MESH)
 
     sends = []
@@ -268,38 +269,33 @@
             for cp in self.last_leg:
                 cp.wait_recv()
 
-    def gather(chunks):
-        parts = [Gather(chunk) for chunk in chunks]
-        for p in parts:
-            p.forward()
-        for p in parts:
-            p.finish()
-
     pl.semaphore_wait(far_ready, 2)
-    gather([lambda i: attn.at[i]])
+    legs = [send(attn.at[z], attn.at[z], at_z(off)) for off in COLUMN]
+    for cp in legs:
+        cp.wait_recv()
 
     opw_cp.wait_recv()
+    heads = attn[...].astype(F32).reshape(NZ, 4, 8, 128)
+    x = jnp.concatenate([heads[:, j].reshape(128, 128) for j in range(4)], axis=1).astype(BF)
+
+    def row_peer(i, row=r):
+        return (row, ey * 4 + lax.rem(ex + i, 4))
+
+    def column_peer(i, row=r):
+        return (row, lax.rem(ey + i, 4) * 4 + ex)
+
+    first_sum = []
+    proj = []
+    for k, peer in ((0, row_peer), (1, column_peer)):
+        proj.append(dot(x, opw[k]))
+        cs1[k] = proj[k].astype(BF)
+        first_sum.append([send(cs1.at[k], cr1.at[k, i - 1], peer(i)) for i in (2, 1, 3)])
     res_cp.wait_recv()
     gain_cp.wait_recv()
     for k in range(2):
         blocks = resb[k].astype(F32).reshape(NZ, 2, 8, 128)
         for t in range(2):
             resf[t, k] = blocks[:, t].reshape(128, 128)
-    heads = attn[...].astype(F32).reshape(NZ, 4, 8, 128)
-    x = jnp.concatenate([heads[:, j].reshape(128, 128) for j in range(4)], axis=1).astype(BF)
-
-    def row_peer(i, row=r):
-        return (row, ey * 4 + lax.rem(ex + i, 4))
-
-    def column_peer(i, row=r):
-        return (row, lax.rem(ey + i, 4) * 4 + ex)
-
-    first_sum = []
-    proj = []
-    for k, peer in ((0, row_peer), (1, column_peer)):
-        proj.append(dot(x, opw[k]))
-        cs1[k] = proj[k].astype(BF)
-        first_sum.append([send(cs1.at[k], cr1.at[k, i - 1], peer(i)) for i in (2, 1, 3)])
     second_sum = []
     for k, peer in ((0, column_peer), (1, row_peer)):
         for cp in first_sum[k]:
@@ -322,7 +318,6 @@
         nb[mine_rows, 128 * k:128 * k + 128] = (h * gainb[k, 0:1, :]).astype(BF)
     nb[mine_rows, 256:384] = hi_lo(jnp.sum(square, axis=1, keepdims=True), 128)
     nb_cp = send(nb.at[mine_rows], nb.at[mine_rows], sibling)
-    hid_cp = send(hid.at[c, oc], hid.at[c, oc], sibling)
 
     for cp in weights:
         cp.wait()
@@ -332,7 +327,7 @@
     rows_in = dot(sel_in[...], nb[...])
     part[:, SQ] = hi_lo(from_hi_lo(rows_in[:, 256:384]), SLOTS)
     rows_in = rows_in[:, :256].astype(BF)
-    for h in range(2):
+    def multiply(h):
         units = slice(QUART * h, QUART * h + QUART)
         for k in range(2):
             here = slice(128 * k, 128 * k + 128)
@@ -351,12 +346,14 @@
         right_cp[h, k] = send(part.at[rows_of(z - 1 - CENTERS[k]), PIECE[h]], from_right.at[k, :, PIECE[h]], at_z(-1))
 
     for h in range(2):
+        multiply(h)
         far_cp[h] = send(part.at[rows_of(z + 8), PIECE[h]], from_far.at[:, PIECE[h]], at_z(-2 * way))
         for k in (0, 4):
             collect(h, k)
     for h in range(2):
         for k in (1, 3):
             collect(h, k)
+    hid_cp = send(hid.at[c, oc], hid.at[c, oc], sibling)
 
     def collected(h, k):
         left_cp[h, k].wait_recv()
@@ -409,10 +406,6 @@
         p.finish()
 
     wd_cp.wait_recv()
-    for k in range(2):
-        down = jnp.concatenate([dot(act[128 * x2:128 * x2 + 128, :], wd[x2, k]) for x2 in range(2)], axis=0)
-        mo[k] = dot(sel_out[...], (down * slot_w[...]).astype(BF)).astype(BF)
-
     def rows_for(other):
         return pl.ds(pl.multiple_of(16 * other, 16), 16)
 
@@ -421,20 +414,22 @@
             mo.at[core, rows_for(other)], fr.at[2 * e + c], bulk_s.at[1], bulk_r.at[1], (2 * z + core, other)
         ).start()
 
-    for step in PLANE:
-        for core in (c, oc):
-            out_send(plane(step), core)
+    for k in range(2):
+        down = jnp.concatenate([dot(act[128 * x2:128 * x2 + 128, :], wd[x2, k]) for x2 in range(2)], axis=0)
+        mo[k] = dot(sel_out[...], (down * slot_w[...]).astype(BF)).astype(BF)
+        for step in PLANE:
+            out_send(plane(step), k)
     out_send(e, oc)
     fr[2 * e + c] = mo[c, rows_for(e)]
+    for cp in sends:
+        cp.wait_send()
+    pltpu.make_async_copy(acc_in.at[pl.ds(0, NE - 1)], acc_in.at[pl.ds(0, NE - 1)], bulk_s.at[0]).wait()
     first_rows = pl.ds(pl.multiple_of(8 * e, 8), 8)
     hid_cp.wait_recv()
     base = jnp.concatenate([hid[0, c, first_rows], hid[1, c, first_rows]], axis=0)
     pltpu.make_async_copy(fr.at[pl.ds(0, 2 * NE - 1)], fr.at[pl.ds(0, 2 * NE - 1)], bulk_r.at[1]).wait()
     o_ref[...] = (base + jnp.sum(fr[...].astype(F32), axis=0)).astype(BF)
 
-    for cp in sends:
-        cp.wait_send()
-    pltpu.make_async_copy(acc_in.at[pl.ds(0, NE - 1)], acc_in.at[pl.ds(0, NE - 1)], bulk_s.at[0]).wait()
     pltpu.make_async_copy(fr.at[pl.ds(0, 2 * NE - 1)], fr.at[pl.ds(0, 2 * NE - 1)], bulk_s.at[1]).wait()
 
 

time: 78.8 us -> 76.4 us (0.970)
  Pallas kernels: 77.4 us -> 75 us
    pallas_call x1, Pallas kernels: 77.4 us -> 75 us  [layer(): pl.pallas_call(kernel, name='layer', out_shape=jax.ShapeDtypeStruct((16,...]
where the time goes in v3:
time: 76.4 us; the launch traced here: 76.3 us
  Pallas kernels  75 us (98%)
  local copies, waits for them, and re-layouts  1.28 us (2%)
    pallas_call x1, Pallas kernels, layer(): pl.pallas_call(kernel, name='layer', out_shape=jax.ShapeDtypeStruct((16,...  75 us

profile of v3, /device:TPU:1, one launch (start us, length us, event | category | flops | bytes accessed | tf_op | source)
XLA Modules:
  0.0 76.3 jit_solution(9974097698786821441)
XLA Ops:
  0.0 75.0 %layer.1 = bf16[16,128]{1,0:T(8,128)(2,1)} custom-call(s32[64]{0:T(128)} %len_hbm.1, bf16[8,8192]{1,0:T(8,128)(2,1)} %q_hbm.1, bf16[8,512]{1,0:T(8,128)(2,1)} %nk_hbm.1, bf16[8,512]{1,0:T(8,128)(2,1)} %nv_hbm.1, bf16[2,384,512]{2,1,0:T(8,128)(2,1)} %bitcast.5, bf16[2,384,512]{2,1,0:T(8,128)(2,1)} %bitcast.6, bf16[512,128]{1,0:T(8,128)(2,1)} %op_ref.1, ...), custom_call_target="tpu_custom_call" | custom-call | tf_op jit(solution)/shard_map/layer/pallas_call | solution.py:454
  75.0 1.3 %copy.16 = bf16[16,128]{1,0:T(8,128)(2,1)} copy(bf16[16,128]{1,0:T(8,128)(2,1)} %layer.1) | data formatting | bytes 8192

commit v4 on v3

--- a/solution.py
+++ b/solution.py
@@ -20,11 +20,10 @@
 TOKENS = 256
 HALF = 768
 QUART = HALF // 2
-WIDE = 2 * HALF + 128
-GATE = (slice(0, QUART), slice(WIDE - 2 * QUART, WIDE - QUART))
-UP = (slice(QUART, 2 * QUART), slice(WIDE - QUART, WIDE))
-SQ = slice(2 * QUART, 2 * QUART + 128)
-PIECE = (slice(0, 2 * QUART + 128), slice(2 * QUART + 128, WIDE))
+WIDE = 2 * HALF
+GATE = (slice(0, QUART), slice(2 * QUART, 3 * QUART))
+UP = (slice(QUART, 2 * QUART), slice(3 * QUART, WIDE))
+PIECE = (slice(0, 2 * QUART), slice(2 * QUART, WIDE))
 NEG = -1e30
 EPS = 1e-6
 CENTERS = (-6, -3, 0, 3, 6)
@@ -53,20 +52,10 @@
     return lax.dot_general(a, b, (((1,), (1,)), ((), ())), preferred_element_type=F32)
 
 
-def hi_lo(v, rows):
-    high = v.astype(BF).astype(F32)
-    lane = lax.broadcasted_iota(jnp.int32, (rows, 128), 1)
-    return jnp.where(lane < 64, high, v - high).astype(BF)
-
-
 def split3(v):
     high = v.astype(BF).astype(F32)
     mid = (v - high).astype(BF).astype(F32)
     return [high, mid, v - high - mid]
-
-
-def from_hi_lo(block):
-    return jnp.sum(block, axis=1, keepdims=True) * (1.0 / 64.0)
 
 
 def kernel(
@@ -75,7 +64,7 @@
     len_ref, q_ref, nk_ref, nv_ref, gain_ref, ids_ref, rw_ref,
     kc, vc, opw, resb, gainb, wg, wu, wd, resf,
     acc, acc_in, wt, attn, cs1, cr1, cs2, cr2,
-    nb, hid, sel_in, sel_out, slot_w, part, from_left, from_right, from_far, s2, r2, act, mo, fr,
+    nb, hid, sq_in, sq, sel_in, sel_out, slot_w, part, from_left, from_right, from_far, s2, r2, act, mo, fr,
     loc, snd, rcv, bulk_s, bulk_r, far_ready,
 ):
     r = lax.axis_index("req")
@@ -316,17 +305,17 @@
         hid[c, k] = h
         square = square + h * h
         nb[mine_rows, 128 * k:128 * k + 128] = (h * gainb[k, 0:1, :]).astype(BF)
-    nb[mine_rows, 256:384] = hi_lo(jnp.sum(square, axis=1, keepdims=True), 128)
     nb_cp = send(nb.at[mine_rows], nb.at[mine_rows], sibling)
+    sq_in[z] = jnp.sum(jnp.transpose(square), axis=0, keepdims=True)
+    for off in COLUMN:
+        remote(sq_in.at[z], sq_in.at[z], bulk_s.at[2], bulk_r.at[2], at_z(off)).start()
 
     for cp in weights:
         cp.wait()
     wg_cp.wait_recv()
     wu_cp.wait_recv()
     nb_cp.wait_recv()
-    rows_in = dot(sel_in[...], nb[...])
-    part[:, SQ] = hi_lo(from_hi_lo(rows_in[:, 256:384]), SLOTS)
-    rows_in = rows_in[:, :256].astype(BF)
+    rows_in = dot(sel_in[...], nb[...]).astype(BF)
     def multiply(h):
         units = slice(QUART * h, QUART * h + QUART)
         for k in range(2):
@@ -368,11 +357,7 @@
     hops = {}
 
     def pass_on(h, k, s, off):
-        if h == 0:
-            s2[k, :, 0:2 * QUART] = s[:, 0:2 * QUART].astype(BF)
-            s2[k, :, SQ] = hi_lo(from_hi_lo(s[:, SQ]), 16)
-        else:
-            s2[k, :, PIECE[h]] = s.astype(BF)
+        s2[k, :, PIECE[h]] = s.astype(BF)
         hops[h, k] = send(s2.at[k, :, PIECE[h]], r2.at[k, :, PIECE[h]], at_z(off))
 
     for h in range(2):
@@ -387,14 +372,19 @@
             s = collected(h, k)
             hops[h, before].wait_recv()
             pass_on(h, k, s + r2[before, :, PIECE[h]].astype(F32), off)
+    pltpu.make_async_copy(sq_in.at[pl.ds(0, NZ - 1)], sq_in.at[pl.ds(0, NZ - 1)], bulk_r.at[2]).wait()
+    sq[c] = jnp.sum(sq_in[...], axis=0)
+    sq_cp = send(sq.at[c], sq.at[c], sibling)
+    sq_cp.wait_recv()
+    owned = sel_in[rows_of(z), :].astype(F32)
+    squares = jnp.sum(owned[:, :128] * sq[0] + owned[:, 128:] * sq[1], axis=1, keepdims=True)
+    norm = lax.rsqrt(squares * (1.0 / D) + EPS)
     gathers = []
     for h in range(2):
         s = collected(h, 2)
         for k in (1, 3):
             hops[h, k].wait_recv()
             s = s + r2[k, :, PIECE[h]].astype(F32)
-        if h == 0:
-            norm = lax.rsqrt(from_hi_lo(s[:, SQ]) * (1.0 / D) + EPS)
         gate = norm * s[:, 0:QUART]
         up = norm * s[:, QUART:2 * QUART]
         units = slice(QUART * h, QUART * h + QUART)
@@ -424,6 +414,7 @@
     for cp in sends:
         cp.wait_send()
     pltpu.make_async_copy(acc_in.at[pl.ds(0, NE - 1)], acc_in.at[pl.ds(0, NE - 1)], bulk_s.at[0]).wait()
+    pltpu.make_async_copy(sq_in.at[pl.ds(0, NZ - 1)], sq_in.at[pl.ds(0, NZ - 1)], bulk_s.at[2]).wait()
     first_rows = pl.ds(pl.multiple_of(8 * e, 8), 8)
     hid_cp.wait_recv()
     base = jnp.concatenate([hid[0, c, first_rows], hid[1, c, first_rows]], axis=0)
@@ -445,12 +436,12 @@
         ((2, 2, 128, HALF), BF), ((2, 2, 128, HALF), BF), ((2, 2, HALF, 128), BF), ((2, 2, 128, 128), F32),
         ((16, 48, 128), BF), ((16, 48, 128), BF), ((128, 128), F32),
         ((16, 32, 128), BF), ((2, 128, 128), BF), ((2, 3, 128, 128), BF), ((2, 128, 128), BF),
-        ((2, 2, 4, 128, 128), BF), ((256, 384), BF), ((2, 2, 128, 128), F32), ((256, 256), BF), ((256, 256), BF), ((256, 128), F32),
+        ((2, 2, 4, 128, 128), BF), ((256, 256), BF), ((2, 2, 128, 128), F32), ((16, 1, 128), F32), ((2, 1, 128), F32), ((256, 256), BF), ((256, 256), BF), ((256, 128), F32),
         ((256, WIDE), BF), ((5, 16, WIDE), BF), ((5, 16, WIDE), BF), ((16, WIDE), BF),
         ((5, 16, WIDE), BF), ((5, 16, WIDE), BF), ((256, HALF), BF),
         ((2, 256, 128), BF), ((32, 16, 128), BF),
     ]
-    sems = [16, 112, 112, 2, 2]
+    sems = [16, 112, 112, 3, 3]
     return pl.pallas_call(
         kernel,
         name="layer",

time: 76.4 us -> 75.3 us (0.986)
  Pallas kernels: 75 us -> 73.8 us
    pallas_call x1, Pallas kernels: 75 us -> 73.8 us  [layer(): pl.pallas_call(kernel, name='layer', out_shape=jax.ShapeDtypeStruct((16,...]
where the time goes in v4:
time: 75.3 us; the launch traced here: 75.1 us
  Pallas kernels  73.8 us (98%)
  local copies, waits for them, and re-layouts  1.28 us (2%)
    pallas_call x1, Pallas kernels, layer(): pl.pallas_call(kernel, name='layer', out_shape=jax.ShapeDtypeStruct((16,...  73.8 us

profile of v4, /device:TPU:1, one launch (start us, length us, event | category | flops | bytes accessed | tf_op | source)
XLA Modules:
  0.0 75.1 jit_solution(12041557924680411776)
XLA Ops:
  0.0 73.8 %layer.1 = bf16[16,128]{1,0:T(8,128)(2,1)} custom-call(s32[64]{0:T(128)} %len_hbm.1, bf16[8,8192]{1,0:T(8,128)(2,1)} %q_hbm.1, bf16[8,512]{1,0:T(8,128)(2,1)} %nk_hbm.1, bf16[8,512]{1,0:T(8,128)(2,1)} %nv_hbm.1, bf16[2,384,512]{2,1,0:T(8,128)(2,1)} %bitcast.5, bf16[2,384,512]{2,1,0:T(8,128)(2,1)} %bitcast.6, bf16[512,128]{1,0:T(8,128)(2,1)} %op_ref.1, ...), custom_call_target="tpu_custom_call" | custom-call | tf_op jit(solution)/shard_map/layer/pallas_call | solution.py:445
  73.8 1.3 %copy.16 = bf16[16,128]{1,0:T(8,128)(2,1)} copy(bf16[16,128]{1,0:T(8,128)(2,1)} %layer.1) | data formatting | bytes 8192

commit v5 on v4

--- a/solution.py
+++ b/solution.py
@@ -342,7 +342,8 @@
     for h in range(2):
         for k in (1, 3):
             collect(h, k)
-    hid_cp = send(hid.at[c, oc], hid.at[c, oc], sibling)
+    first_rows = pl.ds(pl.multiple_of(8 * e, 8), 8)
+    hid_cp = send(hid.at[c, oc, first_rows], hid.at[c, oc, first_rows], sibling)
 
     def collected(h, k):
         left_cp[h, k].wait_recv()
@@ -392,10 +393,14 @@
         gathers.append(Gather(lambda i, units=units: act.at[rows_of(i), units]))
     for p in gathers:
         p.forward()
-    for p in gathers:
+    wd_cp.wait_recv()
+    down = [jnp.zeros((SLOTS, 128), F32)] * 2
+    for h, p in enumerate(gathers):
         p.finish()
-
-    wd_cp.wait_recv()
+        units = slice(QUART * h, QUART * h + QUART)
+        for k in range(2):
+            both = [dot(act[128 * x2:128 * x2 + 128, units], wd[x2, k, units]) for x2 in range(2)]
+            down[k] = down[k] + jnp.concatenate(both, axis=0)
     def rows_for(other):
         return pl.ds(pl.multiple_of(16 * other, 16), 16)
 
@@ -405,8 +410,7 @@
         ).start()
 
     for k in range(2):
-        down = jnp.concatenate([dot(act[128 * x2:128 * x2 + 128, :], wd[x2, k]) for x2 in range(2)], axis=0)
-        mo[k] = dot(sel_out[...], (down * slot_w[...]).astype(BF)).astype(BF)
+        mo[k] = dot(sel_out[...], (down[k] * slot_w[...]).astype(BF)).astype(BF)
         for step in PLANE:
             out_send(plane(step), k)
     out_send(e, oc)
@@ -415,7 +419,6 @@
         cp.wait_send()
     pltpu.make_async_copy(acc_in.at[pl.ds(0, NE - 1)], acc_in.at[pl.ds(0, NE - 1)], bulk_s.at[0]).wait()
     pltpu.make_async_copy(sq_in.at[pl.ds(0, NZ - 1)], sq_in.at[pl.ds(0, NZ - 1)], bulk_s.at[2]).wait()
-    first_rows = pl.ds(pl.multiple_of(8 * e, 8), 8)
     hid_cp.wait_recv()
     base = jnp.concatenate([hid[0, c, first_rows], hid[1, c, first_rows]], axis=0)
     pltpu.make_async_copy(fr.at[pl.ds(0, 2 * NE - 1)], fr.at[pl.ds(0, 2 * NE - 1)], bulk_r.at[1]).wait()

time: 75.3 us -> 75.4 us (level)
  no operation moved by 1% of the time
where the time goes in v5:
time: 75.4 us; the launch traced here: 75.2 us
  Pallas kernels  74 us (98%)
  local copies, waits for them, and re-layouts  1.28 us (2%)
    pallas_call x1, Pallas kernels, layer(): pl.pallas_call(kernel, name='layer', out_shape=jax.ShapeDtypeStruct((16,...  74 us

profile of v5, /device:TPU:1, one launch (start us, length us, event | category | flops | bytes accessed | tf_op | source)
XLA Modules:
  0.0 75.2 jit_solution(14313054596357834017)
XLA Ops:
  0.0 74.0 %layer.1 = bf16[16,128]{1,0:T(8,128)(2,1)} custom-call(s32[64]{0:T(128)} %len_hbm.1, bf16[8,8192]{1,0:T(8,128)(2,1)} %q_hbm.1, bf16[8,512]{1,0:T(8,128)(2,1)} %nk_hbm.1, bf16[8,512]{1,0:T(8,128)(2,1)} %nv_hbm.1, bf16[2,384,512]{2,1,0:T(8,128)(2,1)} %bitcast.5, bf16[2,384,512]{2,1,0:T(8,128)(2,1)} %bitcast.6, bf16[512,128]{1,0:T(8,128)(2,1)} %op_ref.1, ...), custom_call_target="tpu_custom_call" | custom-call | tf_op jit(solution)/shard_map/layer/pallas_call | solution.py:448
  74.0 1.3 %copy.16 = bf16[16,128]{1,0:T(8,128)(2,1)} copy(bf16[16,128]{1,0:T(8,128)(2,1)} %layer.1) | data formatting | bytes 8192
